TPU v7x, 128 devices: a whole 4x4x4 slice. The times are simulated.
128 devices in a mesh: table: 8 (over y, core), seq: 16 (over z, x).
Axes of the slice: x: 4, y: 4, z: 4, core: 2. Of those that a mesh axis runs over, the one named last changes fastest.
Arguments:
- item_ids: int32 [8, 4096], P('table', 'seq'), may hold values from 0 to 524287, as said below
- history_len: int32 [8], P('table'), may hold values from 1024 to 4096, as said below
- row_place: int32 [524288], replicated, may hold values from 0 to 524287, as said below
- item_table: bfloat16 [524288, 512], P(('table', 'seq')), may hold values from -6 to 6
- input_proj: bfloat16 [512, 2048], replicated, may hold values from -0.25 to 0.25
- output_proj: bfloat16 [512, 512], replicated, may hold values from -0.25 to 0.25
- out_cotangent: bfloat16 [8, 4096, 512], P('table', 'seq'), may hold values from -18 to 18
Outputs:
- layer_out: bfloat16 [8, 4096, 512], P('table', 'seq')
- table_grad: bfloat16 [524288, 512], P(('table', 'seq'))
Inputs may be any that keep to these rules, and one draw needn't show every extreme that they name: `item_ids`: within the 256 positions of one device, at most 6 items are stored in any one owner's block of 4096 table rows (rows o * 4096 to (o + 1) * 4096 - 1); one owner's block receives exactly 6 from the positions of every device. `row_place`: A permutation: every table row holds exactly one item. `history_len`: at least one history fills all 4096 positions.
All inputs are finite; a program needn't handle non-finite values.
Results may differ from a plain program's by a relative error of at most 0.006.
Values may be sent and summed in bfloat16 or wider, within the bound.
A program may use at most 128 MiB of HBM per device.

v0:
```python
import math

import jax
import jax.numpy as jnp
from jax import lax
from jax.sharding import PartitionSpec as P

HEADS = 8


eps_norm = 1e-05
block_limit = 512


def dsilu(inputs):
    sigmoid_part = jax.nn.sigmoid(inputs)
    return sigmoid_part * (1.0 + inputs * (1.0 - sigmoid_part))


def normalize(inputs):
    centred = inputs - jnp.mean(inputs, axis=-1, keepdims=True)
    spread = jnp.sqrt(jnp.mean(centred * centred, axis=-1, keepdims=True) + eps_norm)
    return (centred / spread, spread)


def norm_back(gradient, normed, spread):
    mean_grad = jnp.mean(gradient, axis=-1, keepdims=True)
    mean_prod = jnp.mean(gradient * normed, axis=-1, keepdims=True)
    return (gradient - mean_grad - normed * mean_prod) / spread


def heads_view(matrix):
    return matrix.reshape(matrix.shape[0], HEADS, matrix.shape[1] // HEADS)


def tile_mask(query_pos, key_pos, length_user):
    return (key_pos[None, :] <= query_pos[:, None]) & (query_pos[:, None] < length_user)


def tile_forward(queries, keys_blk, values_blk, allowed, score_scale):
    scores = (
        jnp.einsum(
            "lhe,nhe->hln",
            heads_view(queries),
            heads_view(keys_blk),
            preferred_element_type=jnp.float32,
        )
        * score_scale
    )
    weights = jnp.where(allowed[None], jax.nn.silu(scores), 0.0).astype(jnp.bfloat16)
    result = jnp.einsum(
        "hln,nhe->lhe", weights, heads_view(values_blk), preferred_element_type=jnp.float32
    )
    return result.reshape(queries.shape[0], -1)


def tile_query_grad(queries, grad_rows, keys_blk, values_blk, allowed, score_scale):
    scores = (
        jnp.einsum(
            "lhe,nhe->hln",
            heads_view(queries),
            heads_view(keys_blk),
            preferred_element_type=jnp.float32,
        )
        * score_scale
    )
    weight_grad = jnp.einsum(
        "lhe,nhe->hln",
        heads_view(grad_rows),
        heads_view(values_blk),
        preferred_element_type=jnp.float32,
    )
    score_grad = jnp.where(allowed[None], weight_grad * dsilu(scores), 0.0).astype(jnp.bfloat16)
    result = jnp.einsum(
        "hln,nhe->lhe", score_grad, heads_view(keys_blk), preferred_element_type=jnp.float32
    )
    return result.reshape(queries.shape[0], -1) * score_scale


def tile_key_grad(query_piece, grad_piece, keys_mine, values_mine, allowed, score_scale):
    scores = (
        jnp.einsum(
            "lhe,nhe->hln",
            heads_view(query_piece),
            heads_view(keys_mine),
            preferred_element_type=jnp.float32,
        )
        * score_scale
    )
    weights = jnp.where(allowed[None], jax.nn.silu(scores), 0.0).astype(jnp.bfloat16)
    weight_grad = jnp.einsum(
        "lhe,nhe->hln",
        heads_view(grad_piece),
        heads_view(values_mine),
        preferred_element_type=jnp.float32,
    )
    score_grad = jnp.where(allowed[None], weight_grad * dsilu(scores), 0.0).astype(jnp.bfloat16)
    value_part = jnp.einsum(
        "hln,lhe->nhe", weights, heads_view(grad_piece), preferred_element_type=jnp.float32
    )
    key_part = jnp.einsum(
        "hln,lhe->nhe", score_grad, heads_view(query_piece), preferred_element_type=jnp.float32
    )
    key_count = keys_mine.shape[0]
    return (key_part.reshape(key_count, -1) * score_scale, value_part.reshape(key_count, -1))


def over_blocks(tile_fn, running, pieces):
    rows_in = pieces[0].shape[0]
    block_rows = math.gcd(rows_in, block_limit)
    block_count = rows_in // block_rows
    stacked = tuple(
        (member.reshape((block_count, block_rows) + member.shape[1:]) for member in pieces)
    )
    offsets = jnp.arange(block_count, dtype=jnp.int32) * block_rows

    def step_block(carried, scan_item):
        offset, blocks_now = scan_item
        return (tile_fn(carried, blocks_now, offset), None)

    result, unused = lax.scan(step_block, running, (offsets, stacked))
    return result


def local(item_ids, history_len, row_place, item_table, input_proj, output_proj, out_cotangent):
    ids_local = item_ids[0]
    length_user = history_len[0]
    seq_len = ids_local.shape[0]
    rows_dev = item_table.shape[0]
    model_width = item_table.shape[1]
    score_scale = (model_width // HEADS) ** (-0.5)
    table_count = lax.axis_size("table")
    seq_count = lax.axis_size("seq")
    owners = table_count * seq_count
    capacity = 3 * seq_len // owners
    query_first = lax.axis_index("seq") * seq_len
    positions = query_first + jnp.arange(seq_len, dtype=jnp.int32)
    live_rows = (positions < length_user).astype(jnp.float32)[:, None]
    stored = row_place[ids_local]
    owner_of = stored // rows_dev
    local_row = stored % rows_dev
    owner_hits = (owner_of[:, None] == jnp.arange(owners, dtype=jnp.int32)[None, :]).astype(
        jnp.int32
    )
    slot_rank = jnp.sum((jnp.cumsum(owner_hits, axis=0) - owner_hits) * owner_hits, axis=1)
    slot_of = owner_of * capacity + slot_rank
    requests = jnp.full((owners * capacity,), -1, jnp.int32).at[slot_of].set(local_row)
    wanted = lax.all_to_all(
        requests.reshape(owners, capacity),
        ("table", "seq"),
        split_axis=0,
        concat_axis=0,
        tiled=True,
    )
    safe_rows = jnp.maximum(wanted, 0)
    returned = lax.all_to_all(
        jnp.where((wanted >= 0)[..., None], item_table[safe_rows], 0.0),
        ("table", "seq"),
        split_axis=0,
        concat_axis=0,
        tiled=True,
    )
    answered = returned
    asked_rows = wanted
    answered = answered.reshape(owners * capacity, model_width)
    asked_rows = asked_rows.reshape(owners * capacity)
    embedded = answered[slot_of]
    normed_exact, input_spread = normalize(embedded.astype(jnp.float32))
    normed = normed_exact.astype(jnp.bfloat16)
    pre_act = jnp.dot(normed, input_proj, preferred_element_type=jnp.float32)
    activated = jax.nn.silu(pre_act)
    gate_u = activated[:, :model_width]
    values_loc = activated[:, model_width : 2 * model_width].astype(jnp.bfloat16)
    queries_loc = activated[:, 2 * model_width : 3 * model_width].astype(jnp.bfloat16)
    keys_loc = activated[:, 3 * model_width :].astype(jnp.bfloat16)
    zero_rows = jnp.zeros((seq_len, model_width), jnp.float32)

    def forward_tile(running, pieces_blk, key_start):
        keys_blk, values_blk = pieces_blk
        key_pos = key_start + jnp.arange(keys_blk.shape[0], dtype=jnp.int32)
        allowed = tile_mask(positions, key_pos, length_user)
        return running + tile_forward(queries_loc, keys_blk, values_blk, allowed, score_scale)

    attention = over_blocks(
        forward_tile,
        zero_rows,
        (
            lax.all_gather(keys_loc, "seq", axis=0, tiled=True),
            lax.all_gather(values_loc, "seq", axis=0, tiled=True),
        ),
    )
    attn_normed, attn_spread = normalize(attention)
    mixed = (attn_normed * gate_u).astype(jnp.bfloat16)
    branch = jnp.dot(mixed, output_proj, preferred_element_type=jnp.float32)
    layer_out = (live_rows * (embedded.astype(jnp.float32) + branch)).astype(jnp.bfloat16)
    cot_masked = jnp.where(live_rows > 0.0, out_cotangent[0], 0.0)
    mixed_grad = jnp.einsum(
        "ld,ed->le", cot_masked, output_proj, preferred_element_type=jnp.float32
    )
    attention_grad = norm_back(mixed_grad * gate_u, attn_normed, attn_spread).astype(jnp.bfloat16)

    def query_tile(running, pieces_blk, key_start):
        keys_blk, values_blk = pieces_blk
        key_pos = key_start + jnp.arange(keys_blk.shape[0], dtype=jnp.int32)
        allowed = tile_mask(positions, key_pos, length_user)
        return running + tile_query_grad(
            queries_loc, attention_grad, keys_blk, values_blk, allowed, score_scale
        )

    query_grad = over_blocks(
        query_tile,
        zero_rows,
        (
            lax.all_gather(keys_loc, "seq", axis=0, tiled=True),
            lax.all_gather(values_loc, "seq", axis=0, tiled=True),
        ),
    )

    def key_tile(running, pieces_blk, query_start):
        query_piece, grad_piece = pieces_blk
        rows_in = query_piece.shape[0]
        query_pos = query_start + jnp.arange(rows_in, dtype=jnp.int32)
        allowed = tile_mask(query_pos, positions, length_user)
        key_part, value_part = tile_key_grad(
            query_piece, grad_piece, keys_loc, values_loc, allowed, score_scale
        )
        return (running[0] + key_part, running[1] + value_part)

    key_grad, value_grad = over_blocks(
        key_tile,
        (zero_rows, zero_rows),
        (
            lax.all_gather(queries_loc, "seq", axis=0, tiled=True),
            lax.all_gather(attention_grad, "seq", axis=0, tiled=True),
        ),
    )
    activated_grad = jnp.concatenate(
        [mixed_grad * attn_normed, value_grad, query_grad, key_grad], axis=1
    )
    pre_grad = (activated_grad * dsilu(pre_act)).astype(jnp.bfloat16)
    norm_grad = jnp.einsum("lf,df->ld", pre_grad, input_proj, preferred_element_type=jnp.float32)
    embed_grad = cot_masked.astype(jnp.float32) + norm_back(norm_grad, normed_exact, input_spread)
    outgoing = jnp.zeros((owners * capacity, model_width), jnp.float32).at[slot_of].set(embed_grad)
    arrived = lax.all_to_all(
        outgoing.reshape(owners, capacity, model_width).astype(jnp.bfloat16),
        ("table", "seq"),
        split_axis=0,
        concat_axis=0,
        tiled=True,
    ).astype(jnp.float32)
    arrived = arrived.reshape(owners * capacity, model_width)
    arrived = jnp.where((asked_rows >= 0)[:, None], arrived, 0.0)
    table_sum = (
        jnp.zeros((rows_dev, model_width), jnp.float32).at[jnp.maximum(asked_rows, 0)].add(arrived)
    )
    return (layer_out[None], table_sum.astype(jnp.bfloat16))


def solution(mesh):
    placed = (
        P("table", "seq"),
        P("table"),
        P(),
        P(("table", "seq"), None),
        P(),
        P(),
        P("table", "seq", None),
    )
    return jax.shard_map(
        local,
        mesh=mesh,
        in_specs=placed,
        out_specs=(P("table", "seq", None), P(("table", "seq"), None)),
        check_vma=False,
    )
```

profile of v0, /device:TPU:1, one launch (start us, length us, event | category | flops | bytes accessed | tf_op | source)
XLA Modules:
  0.0 639.1 jit_solution(17129103487321654110)
XLA Ops:
  13.7 21.1 %all_to_all.19 = s32[128,1,6]{2,1,0:T(1,128)S(1)} all-to-all(s32[128,1,6]{2,1,0:T(1,128)S(1)} %bitcast.235), channel_id=1, replica_groups=mesh['table'=8,'seq'=16] {'table','seq'}, dimensions={0} | all-to-all | bytes 6144 | tf_op jit(solution)/shard_map/all_to_all | solution.py:148
  36.3 5.4 gather_fusion.1
  45.5 5.2 all-to-all-start.1
  50.8 19.0 %all-to-all-done.1 = bf16[128,6,512]{2,1,0:T(8,128)(2,1)} async-done(((bf16[128,6,512]{2,1,0:T(8,128)(2,1)}), bf16[128,6,512]{2,1,0:T(8,128)(2,1)}, u32[]{:S(2)}, u32[]{:S(2)}) %all-to-all-start.1) | async-done | bytes 786464 | tf_op jit(solution)/shard_map/all_to_all | solution.py:156
  83.4 40.5 %all-gather.5.cloned.1.call-done = bf16[4096,512]{1,0:T(8,128)(2,1)} async-done(((bf16[256,512]{1,0:T(8,128)(2,1)}), bf16[4096,512]{1,0:T(8,128)(2,1)}) %all-gather.5.cloned.1.call-update) | async-done | bytes 4194320 | tf_op jit(solution)/shard_map/all_gather | solution.py:189
  124.0 6.4 %copy.71 = bf16[8,512,512]{1,2,0:T(8,128)(2,1)} copy(bf16[8,512,512]{2,1,0:T(8,128)(2,1)} %bitcast.227) | data formatting | bytes 8388608
  130.4 47.0 %all-gather.7.cloned.1.call-done = bf16[4096,512]{1,0:T(8,128)(2,1)} async-done(((bf16[256,512]{1,0:T(8,128)(2,1)}), bf16[4096,512]{1,0:T(8,128)(2,1)}) %all-gather.7.cloned.1.call-update) | async-done | bytes 4194320 | tf_op jit(solution)/shard_map/all_gather | solution.py:188
  177.4 6.5 %copy.72 = bf16[8,512,512]{1,2,0:T(8,128)(2,1)} copy(bf16[8,512,512]{2,1,0:T(8,128)(2,1)} %bitcast.228) | data formatting | bytes 8388608
  183.8 79.6 %while.35 = (s32[]{:T(128)}, f32[256,512]{0,1:T(8,128)S(1)}, bf16[8,512,512]{1,2,0:T(8,128)(2,1)}, s32[8]{0:T(128)}, s32[]{:T(128)}, /*index=5*/bf16[8,512,512]{...) while((s32[]{:T(128)}, f32[256,512]{0,1:T(8,128)S(1)}, ...), condition=%wide.region_7.8_spmd.clone, body=%wide.region_6.7_spmd.clone.sunk | while | flops 276301056 | bytes 5773967 | solution.py:121
  270.8 120.8 %while.37 = (s32[]{:T(128)}, f32[256,512]{0,1:T(8,128)S(1)}, bf16[8,512,512]{1,2,0:T(8,128)(2,1)}, s32[8]{0:T(128)}, s32[]{:T(128)}, /*index=5*/bf16[8,512,512]{...) while((s32[]{:T(128)}, f32[256,512]{0,1:T(8,128)S(1)}, ...), condition=%wide.region_15.16_spmd.clone, body=%wide.region_14.15_spmd.clone.sunk | while | flops 414844160 | bytes 14949015 | solution.py:121
  279.2 5.6 fusion.144
  294.4 5.5 fusion.144
  309.5 5.6 fusion.144
  324.7 5.5 fusion.144
  339.8 5.4 fusion.144
  354.8 5.5 fusion.144
  369.9 5.4 fusion.144
  384.9 5.4 fusion.144
  392.6 177.3 %while.36 = (s32[]{:T(128)}, f32[256,512]{0,1:T(8,128)}, f32[256,512]{0,1:T(8,128)}, bf16[8,512,512]{2,1,0:T(8,128)(2,1)}, s32[8]{0:T(128)}, /*index=5*/s32[]{:T...) while((s32[]{:T(128)}, f32[256,512]{0,1:T(8,128)}, ...), condition=%wide.region_13.14_spmd.clone, body=%wide.region_12.13_spmd.clone.sunk | while | flops 556664576 | bytes 32382224 | solution.py:121
  402.4 5.5 fusion.137
  424.5 5.5 fusion.137
  430.0 4.6 fusion.136
  446.7 5.5 fusion.137
  468.8 5.5 fusion.137
  491.0 5.5 fusion.137
  513.1 5.5 fusion.137
  535.2 5.5 fusion.137
  557.4 5.5 fusion.137
  584.4 8.1 %all-to-all-start.2 = ((bf16[128,6,512]{2,1,0:T(8,128)(2,1)}), bf16[128,6,512]{2,1,0:T(8,128)(2,1)}, u32[]{:S(2)}, u32[]{:S(2)}) async-start(bf16[128,6,512]{2,1,0:T(8,128)(2,1)} %convert_element_type.79), calls=%async_computation.2 | async-start | bytes 2097152 | tf_op jit(solution)/shard_map/all_to_all | solution.py:244
  595.0 16.4 %all-to-all-done.2 = bf16[128,6,512]{2,1,0:T(8,128)(2,1)} async-done(((bf16[128,6,512]{2,1,0:T(8,128)(2,1)}), bf16[128,6,512]{2,1,0:T(8,128)(2,1)}, u32[]{:S(2)}, u32[]{:S(2)}) %all-to-all-start.2) | async-done | bytes 786464 | tf_op jit(solution)/shard_map/all_to_all | solution.py:244
  613.8 12.8 %scatter_custom_fusion.2 = f32[4096,512]{1,0:T(8,128)} fusion(s32[768]{0:T(1024)} %copy-done.12, f32[]{:T(128)} %constant.119.clone.1, f32[768,512]{1,0:T(8,128)} %reshape.445, pred[768]{0:T(1024)(128)(4,1)S(1)} %ge.20), kind=kCustom, calls=%fused_computation.69 | custom fusion | flops 786432 | bytes 9963264 | tf_op jit(solution)/shard_map/scatter-add | solution.py:254
  626.6 5.9 convert_element_type.80
  (399 shorter events, 336.2 us)
Async XLA Ops:
  7.2 65.6 %copy-start = (bf16[512,2048]{1,0:T(8,128)(2,1)S(1)}, bf16[512,2048]{1,0:T(8,128)(2,1)}, u32[]{:S(2)}) copy-start(bf16[512,2048]{1,0:T(8,128)(2,1)} %param.17) | copy-start | bytes 6291460
  12.1 38.7 %copy-start.17 = (s32[256,1]{0,1:T(1,128)}, s32[256,1]{0,1:T(1,128)S(1)}, u32[]{:S(2)}) copy-start(s32[256,1]{0,1:T(1,128)S(1)} %compare_select_fusion) | copy-start | bytes 3076
  45.5 24.3 %all-to-all-start.1 = ((bf16[128,6,512]{2,1,0:T(8,128)(2,1)}), bf16[128,6,512]{2,1,0:T(8,128)(2,1)}, u32[]{:S(2)}, u32[]{:S(2)}) async-start(bf16[128,6,512]{2,1,0:T(8,128)(2,1)} %broadcast_select_fusion), calls=%async_computation.1 | async-start | bytes 2097152 | tf_op jit(solution)/shard_map/all_to_all | solution.py:156
  50.8 73.2 %all-gather.5.cloned.1.call-start = ((), (), s32[]{:S(2)}) async-start(), calls=%async_computation.3 | async-start | bytes 4456448 | tf_op jit(solution)/shard_map/all_gather | solution.py:189
  76.5 100.9 %all-gather.7.cloned.1.call-start = ((), (), s32[]{:S(2)}) async-start(), calls=%async_computation.4 | async-start | bytes 4456448 | tf_op jit(solution)/shard_map/all_gather | solution.py:188
  77.2 315.4 %all-gather.9.cloned.1.call-start = ((), (), s32[]{:S(2)}) async-start(), calls=%async_computation.5 | async-start | bytes 4456448 | tf_op jit(solution)/shard_map/all_gather | solution.py:233
  78.5 187.4 %copy-start.18 = (pred[256]{0:T(512)(128)(4,1)}, pred[256]{0:T(512)(128)(4,1)S(1)}, u32[]{:S(2)}) copy-start(pred[256]{0:T(512)(128)(4,1)S(1)} %broadcast_compare_fusion.4) | copy-start | bytes 772
  83.2 309.4 %all-gather.11.cloned.1.call-start = ((), (), s32[]{:S(2)}) async-start(), calls=%async_computation.6 | async-start | bytes 4456448 | tf_op jit(solution)/shard_map/all_gather | solution.py:234
  392.6 179.8 %copy-start.14 = (f32[256]{0:T(256)S(1)}, f32[256]{0:T(256)}, u32[]{:S(2)}) copy-start(f32[256]{0:T(256)} %copy-done.13) | copy-start | bytes 3076
  392.6 179.9 %copy-start.16 = (f32[256]{0:T(256)S(1)}, f32[256]{0:T(256)}, u32[]{:S(2)}) copy-start(f32[256]{0:T(256)} %copy-done.15) | copy-start | bytes 3076
  407.9 4.6 copy-start.1
  407.9 4.6 copy-start.3
  430.0 4.6 copy-start.1
  430.0 4.6 copy-start.3
  452.1 4.6 copy-start.1
  452.1 4.6 copy-start.3
  474.3 4.6 copy-start.1
  474.3 4.6 copy-start.3
  496.4 4.6 copy-start.1
  496.4 4.6 copy-start.3
  518.6 4.6 copy-start.1
  518.6 4.6 copy-start.3
  540.7 4.6 copy-start.1
  540.7 4.6 copy-start.3
  562.8 4.6 copy-start.1
  562.8 4.6 copy-start.3
  572.5 3.8 copy-start.8
  572.5 3.8 copy-start.19
  576.3 16.2 %copy-start.11 = (s32[128,1,6]{0,2,1:T(8,128)S(1)}, s32[128,1,6]{0,2,1:T(8,128)}, u32[]{:S(2)}) copy-start(s32[128,1,6]{0,2,1:T(8,128)} %copy-done.10) | copy-start | bytes 9220
  576.3 16.5 %copy-start.6 = (f32[256,512]{1,0:T(8,128)S(1)}, f32[256,512]{1,0:T(8,128)}, u32[]{:S(2)}) copy-start(f32[256,512]{1,0:T(8,128)} %copy.74) | copy-start | bytes 1572868
  579.8 13.0 %copy-start.20 = (bf16[512,512]{1,0:T(8,128)(2,1)S(1)}, bf16[512,512]{1,0:T(8,128)(2,1)}, u32[]{:S(2)}) copy-start(bf16[512,512]{1,0:T(8,128)(2,1)} %param.18) | copy-start | bytes 1572868
  584.4 27.0 %all-to-all-start.2 = ((bf16[128,6,512]{2,1,0:T(8,128)(2,1)}), bf16[128,6,512]{2,1,0:T(8,128)(2,1)}, u32[]{:S(2)}, u32[]{:S(2)}) async-start(bf16[128,6,512]{2,1,0:T(8,128)(2,1)} %convert_element_type.79), calls=%async_computation.2 | async-start | bytes 2097152 | tf_op jit(solution)/shard_map/all_to_all | solution.py:244
  (23 other events, 28.9 us)
Sparse Core Ops, SparseCore 0:
  76.6 47.3 all-gather.4
  126.1 51.2 all-gather.6
  179.5 51.2 all-gather.8
  270.9 51.2 all-gather.10
where the time goes:
time: 644 us; the launch traced here: 639 us
  matrix products  216 us (34%)
  local copies, waits for them, and re-layouts  143 us (22%)
  waiting for transfers between devices  124 us (19%)
  other arithmetic  104 us (16%)
  blocking collectives  21.1 us (3%)
  between operations  14.9 us (2%)
  starting transfers between devices  13.7 us (2%)
    dynamic_slice x72, local copies, waits for them, and re-layouts, over_blocks(): result, unused = lax.scan(step_block, running, (offsets, stacked))  90.7 us
    all_gather x1, waiting for transfers between devices, local(): lax.all_gather(keys_loc, 'seq', axis=0, tiled=True)  47 us
    dot_general x8, matrix products, tile_query_grad(): jnp.einsum('hln,nhe->lhe', score_grad, heads_view(keys_blk), preferred_el...  43.9 us
    dot_general x8, matrix products, tile_key_grad(): jnp.einsum('hln,lhe->nhe', score_grad, heads_view(query_piece), preferred...  43.6 us
    all_gather x1, waiting for transfers between devices, local(): lax.all_gather(values_loc, 'seq', axis=0, tiled=True)  40.5 us
    dot_general x8, matrix products, tile_key_grad(): jnp.einsum('hln,lhe->nhe', weights, heads_view(grad_piece), preferred_ele...  36.6 us
    dot_general x8, matrix products, tile_forward(): jnp.einsum('hln,nhe->lhe', weights, heads_view(values_blk), preferred_ele...  30.6 us
    dot_general x8, matrix products, tile_query_grad(): jnp.einsum('lhe,nhe->hln', heads_view(queries), heads_view(keys_blk), pre...  29.1 us
  transfers between devices with their start and end apart: 6, of which 4 were waited for; matrix products, arithmetic and copies ran while one was open for 36% of the time, Pallas kernels for 0%

commit v1 on v0

v1 whole, which is shorter than its diff:
```python
import functools

import jax
import jax.numpy as jnp
from jax import lax
from jax.experimental import pallas as pl
from jax.experimental.pallas import tpu as pltpu
from jax.sharding import PartitionSpec as P

HEADS = 8
CAP = 6
EPS = 1e-05
F32 = jnp.float32
BF = jnp.bfloat16
MESH = pl.DeviceIdType.MESH
VM = pl.BlockSpec(memory_space=pltpu.VMEM)
SM = pl.BlockSpec(memory_space=pltpu.SMEM)
TABLE, SEQ = 8, 16
OWNERS = TABLE * SEQ
LEN = 256
HD = 64
WIDTH = 512
PIECES = CAP * WIDTH // 128
CHUNK = 2 * LEN
CHUNKS = SEQ // 2
VMEM_LIMIT = 56 * 2**20


def nn(a, b):
    return lax.dot_general(a, b, (((1,), (0,)), ((), ())), preferred_element_type=F32)


def nt(a, b):
    return lax.dot_general(a, b, (((1,), (1,)), ((), ())), preferred_element_type=F32)


def iota(shape, dim):
    return lax.broadcasted_iota(jnp.int32, shape, dim)


def silu(x):
    u = 0.5 * x
    return u + u * jnp.tanh(u)


def dsilu(x):
    u = 0.5 * x
    th = jnp.tanh(u)
    return (0.5 + 0.5 * th) * (1.0 + u * (1.0 - th))


def mean_last(x):
    return jnp.mean(x, axis=-1, keepdims=True)


def normalize(x):
    centred = x - mean_last(x)
    spread = jnp.sqrt(mean_last(centred * centred) + EPS)
    return centred / spread, spread


def norm_back(gradient, normed, spread):
    return (gradient - mean_last(gradient) - normed * mean_last(gradient * normed)) / spread


def places():
    t = lax.axis_index("table")
    s = lax.axis_index("seq")
    return t, s


def barrier_all():
    t, s = places()
    me = t * SEQ + s
    sem = pltpu.get_barrier_semaphore()

    def body(i, carry):
        d = lax.rem(me + i, OWNERS)
        pl.semaphore_signal(
            sem, inc=1, device_id=(d // SEQ, lax.rem(d, SEQ)), device_id_type=MESH
        )
        return carry

    lax.fori_loop(1, OWNERS, body, 0)
    pl.semaphore_wait(sem, OWNERS - 1)


def barrier_plane():
    t, s = places()
    base = t // 2 * 2
    me = lax.rem(t, 2) * SEQ + s
    sem = pltpu.get_barrier_semaphore()

    def body(i, carry):
        d = lax.rem(me + i, 2 * SEQ)
        pl.semaphore_signal(
            sem, inc=1, device_id=(base + d // SEQ, lax.rem(d, SEQ)), device_id_type=MESH
        )
        return carry

    lax.fori_loop(1, 2 * SEQ, body, 0)
    pl.semaphore_wait(sem, 2 * SEQ - 1)


def remote(src, dst, send_sem, recv_sem, t, s):
    return pltpu.make_async_remote_copy(
        src_ref=src,
        dst_ref=dst,
        send_sem=send_sem,
        recv_sem=recv_sem,
        device_id=(t, s),
        device_id_type=MESH,
    )


def wait_bytes(ref, sem):
    pltpu.make_async_copy(ref, ref, sem).wait()


def all_to_all(out_ref, in_ref, send_sem, recv_sem, group_ready):
    t, s = places()
    me = t * SEQ + s

    def group(g, carry):
        tt = lax.rem(t + g, TABLE)
        group_ready(tt)

        def one(i, carry2):
            ss = lax.rem(s + i, SEQ)
            d = tt * SEQ + ss

            @pl.when(d != me)
            def _():
                remote(out_ref.at[d], in_ref.at[me], send_sem, recv_sem, tt, ss).start()

            return carry2

        lax.fori_loop(0, SEQ, one, 0)
        return carry

    lax.fori_loop(0, TABLE, group, 0)
    in_ref[me] = out_ref[me]


def all_to_all_wait(out_ref, in_ref, send_sem, recv_sem):
    wait_bytes(in_ref.at[pl.ds(0, OWNERS - 1)], recv_sem)
    wait_bytes(out_ref.at[pl.ds(0, OWNERS - 1)], send_sem)


def rows_kernel(
    ids_ref, table_ref, ans_ref, want_ref, all_ids, ids2d, acc, spread_buf, outbuf, sems
):
    t, s = places()
    me = t * SEQ + s
    rows_dev = table_ref.shape[0]
    all_ids[me] = ids_ref[...]
    barrier_all()

    def plane(i, carry):
        ss = lax.rem(s + i, SEQ)
        remote(all_ids.at[me], all_ids.at[me], sems.at[0], sems.at[1], t, ss).start()
        return carry

    lax.fori_loop(1, SEQ, plane, 0)
    wait_bytes(all_ids.at[pl.ds(0, SEQ - 1)], sems.at[1])
    mine = all_ids.at[pl.ds(t * SEQ, SEQ)]

    def column(i, carry):
        tt = lax.rem(t + i, TABLE)
        remote(mine, mine, sems.at[2], sems.at[3], tt, s).start()
        return carry

    lax.fori_loop(1, TABLE, column, 0)
    wait_bytes(all_ids.at[pl.ds(0, (TABLE - 1) * SEQ)], sems.at[3])

    def flat(b, carry):
        ids2d[pl.ds(b, 1), :] = all_ids[b]
        return carry

    lax.fori_loop(0, OWNERS, flat, 0, unroll=8)
    ids = ids2d[...]
    hit = ids // rows_dev == me
    local_row = lax.rem(ids, rows_dev).astype(F32)
    before = (iota((LEN, LEN), 0) < iota((LEN, LEN), 1)).astype(BF)
    rank = nn(hit.astype(BF), before)
    value = jnp.where(hit, local_row + 1.0, 0.0)
    wanted = []
    for r in range(CAP):
        got = jnp.sum(jnp.where(rank == r, value, 0.0), axis=1, keepdims=True) - 1.0
        wanted.append(got.astype(jnp.int32))
    lane = iota((OWNERS, OWNERS), 1)
    square = jnp.full((OWNERS, OWNERS), -1.0, F32)
    for r in range(CAP):
        square = jnp.where(lane == r, wanted[r].astype(F32), square)
    want_ref[...] = square.T[:8].astype(jnp.int32)

    block = 512

    def gather(j, carry):
        base = j * block
        table_blk = table_ref[pl.ds(pl.multiple_of(base, block), block), :]
        cols = iota((OWNERS, block), 1) + base
        pick = jnp.concatenate([(w == cols).astype(F32).astype(BF) for w in wanted], axis=0)
        part = nn(pick, table_blk)

        @pl.when(j == 0)
        def _():
            acc[...] = part

        @pl.when(j > 0)
        def _():
            acc[...] += part

        return carry

    lax.fori_loop(0, rows_dev // block, gather, 0)
    for r in range(CAP):
        for q in range(WIDTH // 128):
            spread_buf[pl.ds(r * 4 + q, OWNERS, stride=PIECES), :] = acc[
                r * OWNERS : (r + 1) * OWNERS, q * 128 : (q + 1) * 128
            ]

    def group_ready(tt):
        rows = SEQ * PIECES
        chunk = spread_buf[pl.ds(pl.multiple_of(tt * rows, rows), rows), :]
        outbuf[pl.ds(tt * SEQ, SEQ)] = chunk.astype(BF).reshape(SEQ, PIECES, 128)

    all_to_all(outbuf, ans_ref, sems.at[4], sems.at[5], group_ready)
    wait_bytes(all_ids.at[pl.ds(0, SEQ - 1)], sems.at[0])
    wait_bytes(all_ids.at[pl.ds(0, (TABLE - 1) * SEQ)], sems.at[2])
    all_to_all_wait(outbuf, ans_ref, sems.at[4], sems.at[5])


def fetch_rows(stored_row, item_table):
    return pl.pallas_call(
        rows_kernel,
        out_shape=(
            jax.ShapeDtypeStruct((OWNERS, PIECES, 128), BF),
            jax.ShapeDtypeStruct((8, OWNERS), jnp.int32),
        ),
        in_specs=[VM, VM],
        out_specs=(VM, VM),
        scratch_shapes=[
            pltpu.VMEM((OWNERS, 1, LEN), jnp.int32),
            pltpu.VMEM((OWNERS, LEN), jnp.int32),
            pltpu.VMEM((CAP * OWNERS, WIDTH), F32),
            pltpu.VMEM((OWNERS * PIECES, 128), F32),
            pltpu.VMEM((OWNERS, PIECES, 128), BF),
            pltpu.SemaphoreType.DMA((6,)),
        ],
        compiler_params=pltpu.CompilerParams(
            collective_id=0, has_side_effects=True, vmem_limit_bytes=VMEM_LIMIT
        ),
        name="rows",
    )(stored_row, item_table)


def unpack_rows(packed_ref, spread_buf, rows_buf):
    spread_buf[...] = packed_ref[...].astype(F32).reshape(OWNERS * PIECES, 128)
    for r in range(CAP):
        for q in range(WIDTH // 128):
            rows_buf[r * OWNERS : (r + 1) * OWNERS, q * 128 : (q + 1) * 128] = spread_buf[
                pl.ds(r * 4 + q, OWNERS, stride=PIECES), :
            ].astype(BF)


def query_block(core, k):
    return 2 * k + lax.rem(k + core, 2)


def query_core(s):
    return lax.rem((s + 1) // 2, 2)


def layer_kernel(
    stored_ref, len_ref, ans_ref, win_ref, wo_ref, cot_ref,
    out_ref, grads_ref,
    spread_buf, rows_buf, emb, norm_exact, in_spread, pre, gate, mixed_grad,
    qkv_send, qkv_all, key_nat, value_nat, key_t, value_t,
    o_send, o_all, attn_norm, d_send, d_all,
    dkv_acc, dkv_peer, dkv_send, dkv_all, dq_send, dq_all, qd_pad,
    sem, qkv_sem, relay_sem, d_sem, peer_sem,
):
    t, s = places()
    core = lax.rem(t, 2)
    plane = t - core
    head_user = s // HEADS
    head = lax.rem(s, HEADS)
    owner_t = plane + head_user
    my_user = core
    my_core = query_core(s)
    my_slot = s // 2

    def send(src, dst, send_sem, recv_sem, tt, ss):
        local = (tt == t) & (ss == s)

        @pl.when(local)
        def _():
            pltpu.make_async_copy(src, dst, recv_sem).start()

        @pl.when(jnp.logical_not(local))
        def _():
            remote(src, dst, send_sem, recv_sem, tt, ss).start()

    def sent(src, send_sem, tt, ss):
        @pl.when(jnp.logical_not((tt == t) & (ss == s)))
        def _():
            wait_bytes(src, send_sem)

    unpack_rows(ans_ref, spread_buf, rows_buf)
    stored = stored_ref[...]
    owner = stored // 4096
    owned = (iota((LEN, OWNERS), 1) == owner).astype(F32)
    earlier = (iota((LEN, LEN), 1) < iota((LEN, LEN), 0)).astype(BF)
    rank = jnp.sum(nn(earlier, owned.astype(BF)) * owned, axis=1, keepdims=True)
    slot = rank.astype(jnp.int32) * OWNERS + owner
    pick = (iota((LEN, CAP * OWNERS), 1) == slot).astype(F32).astype(BF)
    embedded = nn(pick, rows_buf[...])
    emb[...] = embedded
    normed, spread = normalize(embedded)
    norm_exact[...] = normed
    in_spread[...] = jnp.broadcast_to(spread, (LEN, 128))
    pre[...] = nn(normed.astype(BF), win_ref[...])
    for g in range(HEADS // 2):
        for part, (first, scale) in enumerate(((2, 0.0625), (3, 1.0), (1, 1.0))):
            low = first * WIDTH + g * 128
            act = silu(pre[:, low : low + 128]).astype(BF).astype(F32) * scale
            turned = act.T.astype(BF)
            qkv_send[2 * g, part * HD : (part + 1) * HD, :] = turned[:HD]
            qkv_send[2 * g + 1, part * HD : (part + 1) * HD, :] = turned[HD:]

    barrier_plane()

    def send_qkv(i, carry):
        h = lax.rem(i + s, HEADS)
        send(
            qkv_send.at[h], qkv_all.at[s], sem.at[0], qkv_sem.at[my_slot],
            plane + my_core, my_user * HEADS + h,
        )
        return carry

    lax.fori_loop(0, HEADS, send_qkv, 0)

    positions = s * LEN + iota((LEN, 1), 0)
    live = positions < len_ref[0]
    cot = jnp.where(live, cot_ref[...].astype(F32), 0.0)
    mixed_grad[...] = nt(cot.astype(BF), wo_ref[...])
    gate[...] = silu(pre[:, :WIDTH])

    peer = plane + 1 - core

    def relay(k):
        i = query_block(core, k)
        wait_bytes(qkv_all.at[i], qkv_sem.at[k])
        ref = qkv_all.at[i, pl.ds(HD, 2 * HD)]
        remote(ref, ref, sem.at[1], relay_sem.at[k], peer, s).start()

    relay(0)

    def forward(k, carry):
        @pl.when(k < CHUNKS - 1)
        def _():
            relay(k + 1)

        wait_bytes(qkv_all.at[0, pl.ds(HD, 2 * HD)], relay_sem.at[k])
        for half in range(2):
            both = qkv_all[2 * k + half]
            rows = slice(half * LEN, (half + 1) * LEN)
            key_t[k, :, rows] = both[HD : 2 * HD]
            value_t[k, :, rows] = both[2 * HD :]
            key_nat[k, rows, :] = both[HD : 2 * HD].T
            value_nat[k, rows, :] = both[2 * HD :].T
        query = qkv_all[query_block(core, k), :HD]

        def tile(j, allowed):
            u = nn(key_nat[j], query)
            if allowed is not None:
                u = jnp.where(allowed, u, 0.0)
            return nn(value_t[j], (u + u * jnp.tanh(u)).astype(BF))

        total = lax.fori_loop(
            0, k, lambda j, o: o + tile(j, None), jnp.zeros((HD, LEN), F32)
        )
        offset = lax.rem(k + core, 2) * LEN
        allowed = iota((CHUNK, LEN), 0) <= iota((CHUNK, LEN), 1) + offset
        o_send[k] = (total + tile(k, allowed)).astype(BF)
        send(
            o_send.at[k], o_all.at[head], sem.at[2], sem.at[3],
            owner_t, query_block(core, k),
        )
        return carry

    lax.fori_loop(0, CHUNKS, forward, 0)

    wait_bytes(o_all, sem.at[3])
    attention = o_all[...].reshape(WIDTH, LEN).astype(F32).T
    attention = jnp.where(live, attention, 0.0)
    attn, attn_spread = normalize(attention)
    attn_norm[...] = attn
    dz = mixed_grad[...] * gate[...]
    attention_grad = norm_back(dz, attn, attn_spread).astype(BF).astype(F32)
    d_send[...] = (0.5 * attention_grad).T.astype(BF).reshape(HEADS, HD, LEN)

    def send_d(i, carry):
        h = lax.rem(i + s, HEADS)
        send(
            d_send.at[h], d_all.at[my_slot], sem.at[4], d_sem.at[my_slot],
            plane + my_core, my_user * HEADS + h,
        )
        return carry

    lax.fori_loop(0, HEADS, send_d, 0)
    mixed = (attn * gate[...]).astype(BF)
    branch = nn(mixed, wo_ref[...])
    out_ref[...] = jnp.where(live, emb[...] + branch, 0.0).astype(BF)

    dkv_acc[...] = jnp.zeros_like(dkv_acc)
    qd_pad[...] = jnp.zeros_like(qd_pad)

    def reduce_keys(k):
        wait_bytes(dkv_peer.at[k], peer_sem.at[k])
        half = lax.rem(k + core, 2)
        own = dkv_acc[k, pl.ds(pl.multiple_of(half * LEN, LEN), LEN), :]
        dkv_send[k] = (2.0 * (own + dkv_peer[k])).astype(BF)
        send(
            dkv_send.at[k], dkv_all.at[head], sem.at[5], sem.at[6],
            owner_t, query_block(core, k),
        )

    def peer_half(k):
        half = 1 - lax.rem(k + core, 2)
        return dkv_acc.at[k, pl.ds(pl.multiple_of(half * LEN, LEN), LEN)]

    def backward(step, carry):
        k = CHUNKS - 1 - step
        wait_bytes(d_all.at[k], d_sem.at[k])
        query = qkv_all[query_block(core, k), :HD]
        grad = d_all[k]
        qd_pad[:LEN, :HD] = query.T
        qd_pad[LEN:, HD:] = grad.T
        pair = qd_pad[...]

        def tile(j, allowed):
            u = nn(key_nat[j], query)
            dp = nn(value_nat[j], grad)
            th = jnp.tanh(u)
            a = 1.0 + th
            p = u * a
            ds = dp * (a * (1.0 + u * (1.0 - th)))
            if allowed is not None:
                p = jnp.where(allowed, p, 0.0)
                ds = jnp.where(allowed, ds, 0.0)
            p = p.astype(BF)
            ds = ds.astype(BF)
            dkv_acc[j] += nn(ds, pair[:LEN]) + nn(p, pair[LEN:])
            return nn(key_t[j], ds)

        total = lax.fori_loop(
            0, k, lambda j, o: o + tile(j, None), jnp.zeros((HD, LEN), F32)
        )
        offset = lax.rem(k + core, 2) * LEN
        allowed = iota((CHUNK, LEN), 0) <= iota((CHUNK, LEN), 1) + offset
        dq_send[k] = (0.125 * (total + tile(k, allowed))).astype(BF)
        send(
            dq_send.at[k], dq_all.at[head], sem.at[7], sem.at[8],
            owner_t, query_block(core, k),
        )
        remote(peer_half(k), dkv_peer.at[k], sem.at[9], peer_sem.at[k], peer, s).start()

        @pl.when(step > 0)
        def _():
            reduce_keys(k + 1)

        return carry

    lax.fori_loop(0, CHUNKS, backward, 0)
    reduce_keys(0)

    wait_bytes(dq_all, sem.at[8])
    wait_bytes(dkv_all, sem.at[6])

    def pre_grad(first, gradient):
        return (gradient * dsilu(pre[:, first * WIDTH : (first + 1) * WIDTH])).astype(BF)

    def by_head(low):
        return jnp.concatenate(
            [dkv_all[h][:, low : low + HD].astype(F32) for h in range(HEADS)], axis=1
        )

    def back(first, gradient):
        return nt(pre_grad(first, gradient), win_ref[:, first * WIDTH : (first + 1) * WIDTH])

    norm_grad = back(0, mixed_grad[...] * attn_norm[...])
    norm_grad += back(1, by_head(HD))
    norm_grad += back(2, dq_all[...].reshape(WIDTH, LEN).astype(F32).T)
    norm_grad += back(3, by_head(0))
    cot = jnp.where(live, cot_ref[...].astype(F32), 0.0)
    embed_grad = cot + norm_back(norm_grad, norm_exact[...], in_spread[:, :1])
    put = lax.dot_general(
        pick, embed_grad.astype(BF), (((0,), (0,)), ((), ())), preferred_element_type=F32
    )
    for r in range(CAP):
        for q in range(WIDTH // 128):
            spread_buf[pl.ds(r * 4 + q, OWNERS, stride=PIECES), :] = put[
                r * OWNERS : (r + 1) * OWNERS, q * 128 : (q + 1) * 128
            ]
    grads_ref[...] = spread_buf[...].astype(BF).reshape(OWNERS, PIECES, 128)

    def drain(i, carry):
        sent(qkv_send.at[0], sem.at[0], plane + my_core, my_user * HEADS + i)
        sent(d_send.at[0], sem.at[4], plane + my_core, my_user * HEADS + i)
        wait_bytes(qkv_all.at[0, pl.ds(HD, 2 * HD)], sem.at[1])
        wait_bytes(dkv_peer.at[0], sem.at[9])
        block = query_block(core, i)
        sent(o_send.at[0], sem.at[2], owner_t, block)
        sent(dkv_send.at[0], sem.at[5], owner_t, block)
        sent(dq_send.at[0], sem.at[7], owner_t, block)
        return carry

    lax.fori_loop(0, CHUNKS, drain, 0)


def layer(stored_col, length, answers, input_proj, output_proj, cot):
    return pl.pallas_call(
        layer_kernel,
        out_shape=(
            jax.ShapeDtypeStruct((LEN, WIDTH), BF),
            jax.ShapeDtypeStruct((OWNERS, PIECES, 128), BF),
        ),
        in_specs=[VM, SM, VM, VM, VM, VM],
        out_specs=(VM, VM),
        scratch_shapes=[
            pltpu.VMEM((OWNERS * PIECES, 128), F32),
            pltpu.VMEM((CAP * OWNERS, WIDTH), BF),
            pltpu.VMEM((LEN, WIDTH), F32),
            pltpu.VMEM((LEN, WIDTH), F32),
            pltpu.VMEM((LEN, 128), F32),
            pltpu.VMEM((LEN, 4 * WIDTH), F32),
            pltpu.VMEM((LEN, WIDTH), F32),
            pltpu.VMEM((LEN, WIDTH), F32),
            pltpu.VMEM((HEADS, 3 * HD, LEN), BF),
            pltpu.VMEM((SEQ, 3 * HD, LEN), BF),
            pltpu.VMEM((CHUNKS, CHUNK, HD), BF),
            pltpu.VMEM((CHUNKS, CHUNK, HD), BF),
            pltpu.VMEM((CHUNKS, HD, CHUNK), BF),
            pltpu.VMEM((CHUNKS, HD, CHUNK), BF),
            pltpu.VMEM((CHUNKS, HD, LEN), BF),
            pltpu.VMEM((HEADS, HD, LEN), BF),
            pltpu.VMEM((LEN, WIDTH), F32),
            pltpu.VMEM((HEADS, HD, LEN), BF),
            pltpu.VMEM((CHUNKS, HD, LEN), BF),
            pltpu.VMEM((CHUNKS, CHUNK, 2 * HD), F32),
            pltpu.VMEM((CHUNKS, LEN, 2 * HD), F32),
            pltpu.VMEM((CHUNKS, LEN, 2 * HD), BF),
            pltpu.VMEM((HEADS, LEN, 2 * HD), BF),
            pltpu.VMEM((CHUNKS, HD, LEN), BF),
            pltpu.VMEM((HEADS, HD, LEN), BF),
            pltpu.VMEM((2 * LEN, 2 * HD), BF),
            pltpu.SemaphoreType.DMA((10,)),
            pltpu.SemaphoreType.DMA((CHUNKS,)),
            pltpu.SemaphoreType.DMA((CHUNKS,)),
            pltpu.SemaphoreType.DMA((CHUNKS,)),
            pltpu.SemaphoreType.DMA((CHUNKS,)),
        ],
        compiler_params=pltpu.CompilerParams(
            collective_id=1, has_side_effects=True, vmem_limit_bytes=VMEM_LIMIT
        ),
        name="layer",
    )(stored_col, length, answers, input_proj, output_proj, cot)


def grads_kernel(out_ref, in_ref, sems):
    barrier_all()
    all_to_all(out_ref, in_ref, sems.at[0], sems.at[1], lambda tt: None)
    all_to_all_wait(out_ref, in_ref, sems.at[0], sems.at[1])


def exchange_grads(outgoing):
    return pl.pallas_call(
        grads_kernel,
        out_shape=jax.ShapeDtypeStruct(outgoing.shape, outgoing.dtype),
        in_specs=[VM],
        out_specs=VM,
        scratch_shapes=[pltpu.SemaphoreType.DMA((2,))],
        compiler_params=pltpu.CompilerParams(
            collective_id=2, has_side_effects=True, vmem_limit_bytes=VMEM_LIMIT
        ),
        name="grads",
    )(outgoing)


def sum_kernel(block, want_ref, packed_ref, out_ref, spread_buf, rows_buf):
    j = pl.program_id(0)

    @pl.when(j == 0)
    def _():
        unpack_rows(packed_ref, spread_buf, rows_buf)

    rows = iota((block, OWNERS), 0) + j * block
    pick = jnp.concatenate(
        [(want_ref[r : r + 1, :] == rows).astype(F32).astype(BF) for r in range(CAP)], axis=1
    )
    out_ref[...] = nn(pick, rows_buf[...]).astype(BF)


def sum_rows(wanted, arrived, rows_dev):
    block = 512
    return pl.pallas_call(
        functools.partial(sum_kernel, block),
        out_shape=jax.ShapeDtypeStruct((rows_dev, WIDTH), BF),
        grid=(rows_dev // block,),
        in_specs=[
            pl.BlockSpec((8, OWNERS), lambda j: (0, 0)),
            pl.BlockSpec((OWNERS, PIECES, 128), lambda j: (0, 0, 0)),
        ],
        out_specs=pl.BlockSpec((block, WIDTH), lambda j: (j, 0)),
        scratch_shapes=[
            pltpu.VMEM((OWNERS * PIECES, 128), F32),
            pltpu.VMEM((CAP * OWNERS, WIDTH), BF),
        ],
        compiler_params=pltpu.CompilerParams(vmem_limit_bytes=VMEM_LIMIT),
        name="sums",
    )(wanted, arrived)


def local(item_ids, history_len, row_place, item_table, input_proj, output_proj, out_cotangent):
    stored = row_place[item_ids[0]]
    answers, wanted = fetch_rows(stored[None, :], item_table)
    layer_out, outgoing = layer(
        stored[:, None], history_len, answers, input_proj, output_proj, out_cotangent[0]
    )
    arrived = exchange_grads(outgoing)
    table_grad = sum_rows(wanted, arrived, item_table.shape[0])
    return layer_out[None], table_grad


def solution(mesh):
    placed = (
        P("table", "seq"),
        P("table"),
        P(),
        P(("table", "seq"), None),
        P(),
        P(),
        P("table", "seq", None),
    )
    return jax.shard_map(
        local,
        mesh=mesh,
        in_specs=placed,
        out_specs=(P("table", "seq", None), P(("table", "seq"), None)),
        check_vma=False,
    )
```

time: 644 us -> 152 us (0.24)
  matrix products: 216 us -> 0 us
  Pallas kernels: 0 us -> 147 us
  local copies, waits for them, and re-layouts: 143 us -> 3.35 us
  waiting for transfers between devices: 124 us -> 0 us
  other arithmetic: 104 us -> 0.69 us
  blocking collectives: 21.1 us -> 0 us
  starting transfers between devices: 13.7 us -> 0 us
  between operations: 14.9 us -> 1.48 us
    dot_general x52 -> x0, matrix products: 216 us -> none  [the longest x8 43.9 us: tile_query_grad(): jnp.einsum('hln,nhe->lhe', score_grad, heads_view(keys_blk), preferred_el...]
    pallas_call x0 -> x4, Pallas kernels: none -> 147 us  [the longest x1 77.1 us: layer(): pl.pallas_call(layer_kernel, out_shape=(jax.ShapeDtypeStruct((LEN, WIDTH)...]
    dynamic_slice x72 -> x0, local copies, waits for them, and re-layouts: 90.7 us -> none  [over_blocks(): result, unused = lax.scan(step_block, running, (offsets, stacked))]
    all_gather x4 -> x0, waiting for transfers between devices: 87.5 us -> none  [the longest x1 47 us: local(): lax.all_gather(keys_loc, 'seq', axis=0, tiled=True)]
    add x72 -> x0, other arithmetic: 46.8 us -> none  [the longest x8 12.4 us: key_tile(): return (running[0] + key_part, running[1] + value_part)]
    all_to_all x2 -> x0, waiting for transfers between devices: 35.4 us -> none  [the longest x1 19 us: local(): lax.all_to_all(jnp.where((wanted >= 0)[..., None], item_table[safe_rows],...]
    all_to_all x1 -> x0, blocking collectives: 21.1 us -> none  [local(): lax.all_to_all(requests.reshape(owners, capacity), ('table', 'seq'), spli...]
    lt x24 -> x0, other arithmetic: 20.8 us -> none  [tile_mask(): query_pos[:, None] < length_user]
  transfers between devices with their start and end apart: 6 -> 0, of which waited for: 4 -> 0; matrix products, arithmetic and copies ran while one was open for 36% -> 0% of each run, Pallas kernels for 0% -> 0%
where the time goes in v1:
time: 152 us
  Pallas kernels  147 us (97%)
  local copies, waits for them, and re-layouts  3.35 us (2%)
    pallas_call x1, Pallas kernels, layer(): pl.pallas_call(layer_kernel, out_shape=(jax.ShapeDtypeStruct((LEN, WIDTH)...  77.1 us
    pallas_call x1, Pallas kernels, fetch_rows(): pl.pallas_call(rows_kernel, out_shape=(jax.ShapeDtypeStruct((OWNERS, PIEC...  41.4 us
    pallas_call x1, Pallas kernels, exchange_grads(): pl.pallas_call(grads_kernel, out_shape=jax.ShapeDtypeStruct(outgoing.shap...  20.4 us
    pallas_call x1, Pallas kernels, sum_rows(): pl.pallas_call(functools.partial(sum_kernel, block), out_shape=jax.ShapeD...  7.66 us

profile of v1, /device:TPU:1, one launch (start us, length us, event | category | flops | bytes accessed | tf_op | source)
XLA Modules:
  0.0 152.1 jit_solution(3385069611721348032)
XLA Ops:
  0.6 0.0 copy-start
  1.4 0.7 compare_select_fusion
  2.1 0.1 copy-done
  2.2 1.7 %gather_fusion = s32[256]{0:T(256)S(1)} fusion(s32[524288]{0:T(1024)S(1)} %copy-done, s32[1024]{0:T(1024)S(1)} %pad_clamp_fusion), kind=kCustom, calls=%fused_computation | custom fusion | bytes 3072 | tf_op jit(solution)/shard_map/gather | solution.py:627
  4.0 0.0 copy-start.2
  4.0 0.8 copy.9.stored_ref
  4.8 0.0 copy-done.2
  4.8 41.4 %rows.1 = (bf16[128,24,128]{2,1,0:T(8,128)(2,1)}, s32[8,128]{1,0:T(8,128)}) custom-call(s32[1,256]{1,0:T(1,128)} %bitcast.10, bf16[4096,512]{1,0:T(8,128)(2,1)} %table_ref.1), custom_call_target="tpu_custom_call" | custom-call | tf_op jit(solution)/shard_map/rows/pallas_call | solution.py:235
  46.2 77.1 %layer.1 = (bf16[256,512]{1,0:T(8,128)(2,1)}, bf16[128,24,128]{2,1,0:T(8,128)(2,1)}) custom-call(s32[256,1]{1,0:T(8,128)} %copy.9.stored_ref, s32[1]{0:T(128)S(6)} %copy.11.len_ref, bf16[128,24,128]{2,1,0:T(8,128)(2,1)} %get-tuple-element.6.ans_ref, bf16[512,2048]{1,0:T(8,128)(2,1)} %win_ref.1, bf16[512,512]{1,0:T(8,128)(2,1)} %wo_ref.1, ...), custom_call_target="tpu_custom_call" | custom-call | tf_op jit(solution)/shard_map/layer/pallas_call | solution.py:524
  123.3 20.4 %grads.1.packed_ref = bf16[128,24,128]{2,1,0:T(8,128)(2,1)} custom-call(bf16[128,24,128]{2,1,0:T(8,128)(2,1)} %get-tuple-element.9.out_ref), custom_call_target="tpu_custom_call" | custom-call | tf_op jit(solution)/shard_map/grads/pallas_call | solution.py:579
  143.8 0.0 copy-start.1
  143.8 7.7 %sums.1 = bf16[4096,512]{1,0:T(8,128)(2,1)} custom-call(s32[8,128]{1,0:T(8,128)} %get-tuple-element.8.want_ref, bf16[128,24,128]{2,1,0:T(8,128)(2,1)} %grads.1.packed_ref), custom_call_target="tpu_custom_call" | custom-call | tf_op jit(solution)/shard_map/sums/pallas_call | solution.py:608
  151.4 0.0 copy-done.1
  151.4 0.7 copy.12
  (1 shorter events, 0.0 us)
Async XLA Ops:
  0.6 1.6 %copy-start = (s32[524288]{0:T(1024)S(1)}, s32[524288]{0:T(1024)}, u32[]{:S(2)}) copy-start(s32[524288]{0:T(1024)} %param.9) | copy-start | bytes 6291460
  4.0 0.8 copy-start.2
  143.8 7.7 %copy-start.1 = (bf16[256,512]{1,0:T(8,128)(2,1)S(1)}, bf16[256,512]{1,0:T(8,128)(2,1)}, u32[]{:S(2)}) copy-start(bf16[256,512]{1,0:T(8,128)(2,1)} %get-tuple-element.7) | copy-start | bytes 786436

commit v2 on v1

v2 whole, which is shorter than its diff:
```python
import functools

import jax
import jax.numpy as jnp
from jax import lax
from jax.experimental import pallas as pl
from jax.experimental.pallas import tpu as pltpu
from jax.sharding import PartitionSpec as P

HEADS = 8
CAP = 6
EPS = 1e-05
F32 = jnp.float32
BF = jnp.bfloat16
MESH = pl.DeviceIdType.MESH
VM = pl.BlockSpec(memory_space=pltpu.VMEM)
SM = pl.BlockSpec(memory_space=pltpu.SMEM)
TABLE, SEQ = 8, 16
OWNERS = TABLE * SEQ
LEN = 256
HD = 64
WIDTH = 512
PIECES = CAP * WIDTH // 128
CHUNK = 2 * LEN
CHUNKS = SEQ // 2
VMEM_LIMIT = 56 * 2**20


def nn(a, b):
    return lax.dot_general(a, b, (((1,), (0,)), ((), ())), preferred_element_type=F32)


def nt(a, b):
    return lax.dot_general(a, b, (((1,), (1,)), ((), ())), preferred_element_type=F32)


def iota(shape, dim):
    return lax.broadcasted_iota(jnp.int32, shape, dim)


def silu(x):
    u = 0.5 * x
    return u + u * jnp.tanh(u)


def dsilu(x):
    u = 0.5 * x
    th = jnp.tanh(u)
    return (0.5 + 0.5 * th) * (1.0 + u * (1.0 - th))


def mean_last(x):
    return jnp.mean(x, axis=-1, keepdims=True)


def normalize(x):
    centred = x - mean_last(x)
    spread = jnp.sqrt(mean_last(centred * centred) + EPS)
    return centred / spread, spread


def norm_back(gradient, normed, spread):
    return (gradient - mean_last(gradient) - normed * mean_last(gradient * normed)) / spread


def places():
    t = lax.axis_index("table")
    s = lax.axis_index("seq")
    return t, s


def barrier_all():
    t, s = places()
    me = t * SEQ + s
    sem = pltpu.get_barrier_semaphore()

    def body(i, carry):
        d = lax.rem(me + i, OWNERS)
        pl.semaphore_signal(
            sem, inc=1, device_id=(d // SEQ, lax.rem(d, SEQ)), device_id_type=MESH
        )
        return carry

    lax.fori_loop(1, OWNERS, body, 0)
    pl.semaphore_wait(sem, OWNERS - 1)


def remote(src, dst, send_sem, recv_sem, t, s):
    return pltpu.make_async_remote_copy(
        src_ref=src,
        dst_ref=dst,
        send_sem=send_sem,
        recv_sem=recv_sem,
        device_id=(t, s),
        device_id_type=MESH,
    )


def wait_bytes(ref, sem):
    pltpu.make_async_copy(ref, ref, sem).wait()


def unpack_rows(packed_ref, spread_buf, rows_buf):
    spread_buf[...] = packed_ref[...].astype(F32).reshape(OWNERS * PIECES, 128)
    for r in range(CAP):
        for q in range(WIDTH // 128):
            rows_buf[r * OWNERS : (r + 1) * OWNERS, q * 128 : (q + 1) * 128] = spread_buf[
                pl.ds(r * 4 + q, OWNERS, stride=PIECES), :
            ].astype(BF)


def query_block(core, k):
    return 2 * k + lax.rem(k + core, 2)


def query_core(s):
    return lax.rem((s + 1) // 2, 2)


def pack_rows(rows, count, spread_buf, out_ref, first):
    for r in range(CAP):
        for q in range(WIDTH // 128):
            spread_buf[pl.ds(r * 4 + q, count, stride=PIECES), :] = rows[
                r * count : (r + 1) * count, q * 128 : (q + 1) * 128
            ]
    chunk = spread_buf[: count * PIECES, :]
    out_ref[pl.ds(first, count)] = chunk.astype(BF).reshape(count, PIECES, 128)


def layer_kernel(
    ids_ref, stored_ref, len_ref, table_hbm, win_hbm, wo_hbm, cot_hbm,
    out_ref, grads_ref, want_ref,
    table_ref, win_ref, wo_ref, cot_ref, all_ids, ids2d, acc, outbuf, ans_ref,
    spread_buf, rows_buf, emb, norm_exact, in_spread, pre, gate, mixed_grad,
    qkv_send, qkv_all, key_nat, value_nat, key_t, value_t,
    o_send, o_all, attn_norm, d_send, d_all,
    dkv_acc, dkv_peer, dkv_send, dkv_all, dq_send, dq_all, qd_pad,
    load_sem, sem, qkv_sem, relay_sem, d_sem, peer_sem,
):
    t, s = places()
    me = t * SEQ + s
    core = lax.rem(t, 2)
    plane = t - core
    head_user = s // HEADS
    head = lax.rem(s, HEADS)
    owner_t = plane + head_user
    my_user = core
    my_core = query_core(s)
    my_slot = s // 2
    rows_dev = table_ref.shape[0]

    loads = [
        pltpu.make_async_copy(src, dst, load_sem.at[n])
        for n, (src, dst) in enumerate(
            ((table_hbm, table_ref), (win_hbm, win_ref), (wo_hbm, wo_ref), (cot_hbm, cot_ref))
        )
    ]
    for load in loads:
        load.start()
    all_ids[me] = ids_ref[...]
    barrier_all()

    def send(src, dst, send_sem, recv_sem, tt, ss):
        local = (tt == t) & (ss == s)

        @pl.when(local)
        def _():
            pltpu.make_async_copy(src, dst, recv_sem).start()

        @pl.when(jnp.logical_not(local))
        def _():
            remote(src, dst, send_sem, recv_sem, tt, ss).start()

    def sent(src, send_sem, tt, ss):
        @pl.when(jnp.logical_not((tt == t) & (ss == s)))
        def _():
            wait_bytes(src, send_sem)

    def to_plane(i, carry):
        ss = lax.rem(s + i, SEQ)
        remote(all_ids.at[me], all_ids.at[me], sem.at[10], sem.at[11], t, ss).start()
        return carry

    lax.fori_loop(1, SEQ, to_plane, 0)
    wait_bytes(all_ids.at[pl.ds(0, SEQ - 1)], sem.at[11])
    mine = all_ids.at[pl.ds(t * SEQ, SEQ)]

    def to_column(i, carry):
        tt = lax.rem(t + i, TABLE)
        remote(mine, mine, sem.at[12], sem.at[13], tt, s).start()
        return carry

    lax.fori_loop(1, TABLE, to_column, 0)

    stored = stored_ref[...]
    owner = stored // rows_dev
    owned = (iota((LEN, OWNERS), 1) == owner).astype(F32)
    earlier = (iota((LEN, LEN), 1) < iota((LEN, LEN), 0)).astype(BF)
    rank = jnp.sum(nn(earlier, owned.astype(BF)) * owned, axis=1, keepdims=True)
    slot = rank.astype(jnp.int32) * OWNERS + owner
    positions = s * LEN + iota((LEN, 1), 0)
    live = positions < len_ref[0]

    wait_bytes(all_ids.at[pl.ds(0, (TABLE - 1) * SEQ)], sem.at[13])

    def flat(b, carry):
        ids2d[pl.ds(b, 1), :] = all_ids[lax.rem(t * SEQ + b, OWNERS)]
        return carry

    lax.fori_loop(0, OWNERS, flat, 0, unroll=8)
    ids = ids2d[...]
    hit = ids // rows_dev == me
    local_row = lax.rem(ids, rows_dev).astype(F32)
    before = (iota((LEN, LEN), 0) < iota((LEN, LEN), 1)).astype(BF)
    order = nn(hit.astype(BF), before)
    value = jnp.where(hit, local_row + 1.0, 0.0)
    wanted = []
    for r in range(CAP):
        got = jnp.sum(jnp.where(order == r, value, 0.0), axis=1, keepdims=True) - 1.0
        wanted.append(got.astype(jnp.int32))
    lane = iota((OWNERS, OWNERS), 1)
    square = jnp.full((OWNERS, OWNERS), -1.0, F32)
    for r in range(CAP):
        square = jnp.where(lane == r, wanted[r].astype(F32), square)
    want_ref[...] = square.T[:8].astype(jnp.int32)

    block = 512
    half_count = OWNERS // 2
    loads[0].wait()

    def send_group(src_ref, dst_ref, dst_at, send_sem, recv_sem, g):
        tt = lax.rem(t + g, TABLE)

        def one(i, carry):
            ss = lax.rem(s + i, SEQ)

            @pl.when((g > 0) | (i > 0))
            def _():
                remote(
                    src_ref.at[g * SEQ + ss], dst_ref.at[dst_at(tt)], send_sem, recv_sem, tt, ss
                ).start()

            return carry

        lax.fori_loop(0, SEQ, one, 0)

    for half in range(2):
        low = half * half_count

        def gather(j, carry, low=low):
            base = j * block
            table_blk = table_ref[pl.ds(pl.multiple_of(base, block), block), :]
            cols = iota((half_count, block), 1) + base
            pick_rows = jnp.concatenate(
                [(w[low : low + half_count] == cols).astype(F32).astype(BF) for w in wanted], axis=0
            )
            part = nn(pick_rows, table_blk)

            @pl.when(j == 0)
            def _():
                acc[...] = part

            @pl.when(j > 0)
            def _():
                acc[...] += part

            return carry

        lax.fori_loop(0, rows_dev // block, gather, 0)
        pack_rows(acc, half_count, spread_buf, outbuf, low)

        def send_rows(g, carry):
            send_group(outbuf, ans_ref, lambda tt: me, sem.at[14], sem.at[15], g)
            return carry

        lax.fori_loop(half * TABLE // 2, (half + 1) * TABLE // 2, send_rows, 0)
    ans_ref[me] = outbuf[s]
    pick = (iota((LEN, CAP * OWNERS), 1) == slot).astype(F32).astype(BF)
    for load in loads[1:]:
        load.wait()
    cot = jnp.where(live, cot_ref[...].astype(F32), 0.0)
    mixed_grad[...] = nt(cot.astype(BF), wo_ref[...])
    dkv_acc[...] = jnp.zeros_like(dkv_acc)
    qd_pad[...] = jnp.zeros_like(qd_pad)
    wait_bytes(ans_ref.at[pl.ds(0, OWNERS - 1)], sem.at[15])

    unpack_rows(ans_ref, spread_buf, rows_buf)
    embedded = nn(pick, rows_buf[...])
    emb[...] = embedded
    normed, spread = normalize(embedded)
    norm_exact[...] = normed
    in_spread[...] = jnp.broadcast_to(spread, (LEN, 128))
    pre[...] = nn(normed.astype(BF), win_ref[...])
    for g in range(HEADS // 2):
        for part, (first, scale) in enumerate(((2, 0.0625), (3, 1.0), (1, 1.0))):
            low = first * WIDTH + g * 128
            act = silu(pre[:, low : low + 128]).astype(BF).astype(F32) * scale
            turned = act.T.astype(BF)
            qkv_send[2 * g, part * HD : (part + 1) * HD, :] = turned[:HD]
            qkv_send[2 * g + 1, part * HD : (part + 1) * HD, :] = turned[HD:]

    def send_qkv(i, carry):
        h = lax.rem(i + s, HEADS)
        send(
            qkv_send.at[h], qkv_all.at[s], sem.at[0], qkv_sem.at[my_slot],
            plane + my_core, my_user * HEADS + h,
        )
        return carry

    lax.fori_loop(0, HEADS, send_qkv, 0)

    gate[...] = silu(pre[:, :WIDTH])
    pre[...] = dsilu(pre[...])

    peer = plane + 1 - core

    def relay(k):
        i = query_block(core, k)
        wait_bytes(qkv_all.at[i], qkv_sem.at[k])
        ref = qkv_all.at[i, pl.ds(HD, 2 * HD)]
        remote(ref, ref, sem.at[1], relay_sem.at[k], peer, s).start()

    relay(0)

    def may_see(k):
        offset = lax.rem(k + core, 2) * LEN
        return iota((CHUNK, LEN), 0) <= iota((CHUNK, LEN), 1) + offset

    for k in range(CHUNKS):
        if k < CHUNKS - 1:
            relay(k + 1)
        wait_bytes(qkv_all.at[0, pl.ds(HD, 2 * HD)], relay_sem.at[k])
        for half in range(2):
            both = qkv_all[2 * k + half]
            rows = slice(half * LEN, (half + 1) * LEN)
            key_t[k, :, rows] = both[HD : 2 * HD]
            value_t[k, :, rows] = both[2 * HD :]
            key_nat[k, rows, :] = both[HD : 2 * HD].T
            value_nat[k, rows, :] = both[2 * HD :].T
        query = qkv_all[query_block(core, k), :HD]
        total = None
        for j in range(k + 1):
            u = nn(key_nat[j], query)
            if j == k:
                u = jnp.where(may_see(k), u, 0.0)
            part = nn(value_t[j], (u + u * jnp.tanh(u)).astype(BF))
            total = part if total is None else total + part
        o_send[k] = total
        send(
            o_send.at[k], o_all.at[head], sem.at[2], sem.at[3],
            owner_t, query_block(core, k),
        )

    wait_bytes(o_all, sem.at[3])
    attention = o_all[...].reshape(WIDTH, LEN).T
    attention = jnp.where(live, attention, 0.0)
    attn, attn_spread = normalize(attention)
    attn_norm[...] = attn
    dz = mixed_grad[...] * gate[...]
    attention_grad = norm_back(dz, attn, attn_spread).astype(BF).astype(F32)
    d_send[...] = (0.5 * attention_grad).T.astype(BF).reshape(HEADS, HD, LEN)

    def send_d(i, carry):
        h = lax.rem(i + s, HEADS)
        send(
            d_send.at[h], d_all.at[my_slot], sem.at[4], d_sem.at[my_slot],
            plane + my_core, my_user * HEADS + h,
        )
        return carry

    lax.fori_loop(0, HEADS, send_d, 0)
    mixed = (attn * gate[...]).astype(BF)
    branch = nn(mixed, wo_ref[...])
    out_ref[...] = jnp.where(live, emb[...] + branch, 0.0).astype(BF)

    def reduce_keys(k):
        wait_bytes(dkv_peer.at[k], peer_sem.at[k])
        half = lax.rem(k + core, 2)
        own = dkv_acc[k, pl.ds(pl.multiple_of(half * LEN, LEN), LEN), :]
        dkv_send[k] = (2.0 * (own + dkv_peer[k])).astype(BF)
        send(
            dkv_send.at[k], dkv_all.at[head], sem.at[5], sem.at[6],
            owner_t, query_block(core, k),
        )

    def peer_half(k):
        half = 1 - lax.rem(k + core, 2)
        return dkv_acc.at[k, pl.ds(pl.multiple_of(half * LEN, LEN), LEN)]

    for k in range(CHUNKS - 1, -1, -1):
        wait_bytes(d_all.at[k], d_sem.at[k])
        query = qkv_all[query_block(core, k), :HD]
        grad = d_all[k]
        qd_pad[:LEN, :HD] = query.T
        qd_pad[LEN:, HD:] = grad.T
        pair = qd_pad[...]
        total = None
        for j in range(k + 1):
            u = nn(key_nat[j], query)
            dp = nn(value_nat[j], grad)
            th = jnp.tanh(u)
            a = 1.0 + th
            p = u * a
            ds = dp * (a * (1.0 + u * (1.0 - th)))
            if j == k:
                p = jnp.where(may_see(k), p, 0.0)
                ds = jnp.where(may_see(k), ds, 0.0)
            p = p.astype(BF)
            ds = ds.astype(BF)
            dkv_acc[j] += nn(ds, pair[:LEN]) + nn(p, pair[LEN:])
            part = nn(key_t[j], ds)
            total = part if total is None else total + part
        dq_send[k] = (0.125 * total).astype(BF)
        send(
            dq_send.at[k], dq_all.at[head], sem.at[7], sem.at[8],
            owner_t, query_block(core, k),
        )
        remote(peer_half(k), dkv_peer.at[k], sem.at[9], peer_sem.at[k], peer, s).start()
        if k < CHUNKS - 1:
            reduce_keys(k + 1)
    reduce_keys(0)

    def back(first, gradient):
        cols = slice(first * WIDTH, (first + 1) * WIDTH)
        return nt((gradient * pre[:, cols]).astype(BF), win_ref[:, cols])

    def by_head(low):
        return jnp.concatenate(
            [dkv_all[h][:, low : low + HD].astype(F32) for h in range(HEADS)], axis=1
        )

    norm_grad = back(0, mixed_grad[...] * attn_norm[...])
    wait_bytes(dq_all, sem.at[8])
    norm_grad += back(2, dq_all[...].reshape(WIDTH, LEN).astype(F32).T)
    wait_bytes(dkv_all, sem.at[6])
    norm_grad += back(1, by_head(HD))
    norm_grad += back(3, by_head(0))
    cot = jnp.where(live, cot_ref[...].astype(F32), 0.0)
    embed_grad = cot + norm_back(norm_grad, norm_exact[...], in_spread[:, :1])
    wait_bytes(outbuf.at[pl.ds(0, OWNERS - 1)], sem.at[14])
    turned_owner = lax.rem(owner + (OWNERS - t * SEQ), OWNERS)
    turned_slot = rank.astype(jnp.int32) * OWNERS + turned_owner
    put_pick = (iota((LEN, CAP * OWNERS), 1) == turned_slot).astype(F32).astype(BF)
    acc_put = lax.dot_general(
        put_pick, embed_grad.astype(BF), (((0,), (0,)), ((), ())), preferred_element_type=F32
    )
    pack_rows(acc_put, OWNERS, spread_buf, outbuf, 0)

    def send_grads(g, carry):
        send_group(
            outbuf, grads_ref, lambda tt: lax.rem(t - tt + TABLE, TABLE) * SEQ + s,
            sem.at[16], sem.at[17], g,
        )
        return carry

    lax.fori_loop(0, TABLE, send_grads, 0)
    grads_ref[s] = outbuf[s]

    wait_bytes(all_ids.at[pl.ds(0, SEQ - 1)], sem.at[10])
    wait_bytes(all_ids.at[pl.ds(0, (TABLE - 1) * SEQ)], sem.at[12])

    def drain(i, carry):
        sent(qkv_send.at[0], sem.at[0], plane + my_core, my_user * HEADS + i)
        sent(d_send.at[0], sem.at[4], plane + my_core, my_user * HEADS + i)
        wait_bytes(qkv_all.at[0, pl.ds(HD, 2 * HD)], sem.at[1])
        wait_bytes(dkv_peer.at[0], sem.at[9])
        block_now = query_block(core, i)
        sent(o_send.at[0], sem.at[2], owner_t, block_now)
        sent(dkv_send.at[0], sem.at[5], owner_t, block_now)
        sent(dq_send.at[0], sem.at[7], owner_t, block_now)
        return carry

    lax.fori_loop(0, CHUNKS, drain, 0)
    wait_bytes(grads_ref.at[pl.ds(0, OWNERS - 1)], sem.at[17])
    wait_bytes(outbuf.at[pl.ds(0, OWNERS - 1)], sem.at[16])


def layer(stored, length, item_table, input_proj, output_proj, cot):
    anywhere = pl.BlockSpec(memory_space=pl.ANY)
    return pl.pallas_call(
        layer_kernel,
        out_shape=(
            jax.ShapeDtypeStruct((LEN, WIDTH), BF),
            jax.ShapeDtypeStruct((OWNERS, PIECES, 128), BF),
            jax.ShapeDtypeStruct((8, OWNERS), jnp.int32),
        ),
        in_specs=[VM, VM, SM, anywhere, anywhere, anywhere, anywhere],
        out_specs=(VM, VM, VM),
        scratch_shapes=[
            pltpu.VMEM(item_table.shape, BF),
            pltpu.VMEM((WIDTH, 4 * WIDTH), BF),
            pltpu.VMEM((WIDTH, WIDTH), BF),
            pltpu.VMEM((LEN, WIDTH), BF),
            pltpu.VMEM((OWNERS, 1, LEN), jnp.int32),
            pltpu.VMEM((OWNERS, LEN), jnp.int32),
            pltpu.VMEM((CAP * OWNERS // 2, WIDTH), F32),
            pltpu.VMEM((OWNERS, PIECES, 128), BF),
            pltpu.VMEM((OWNERS, PIECES, 128), BF),
            pltpu.VMEM((OWNERS * PIECES, 128), F32),
            pltpu.VMEM((CAP * OWNERS, WIDTH), BF),
            pltpu.VMEM((LEN, WIDTH), F32),
            pltpu.VMEM((LEN, WIDTH), F32),
            pltpu.VMEM((LEN, 128), F32),
            pltpu.VMEM((LEN, 4 * WIDTH), F32),
            pltpu.VMEM((LEN, WIDTH), F32),
            pltpu.VMEM((LEN, WIDTH), F32),
            pltpu.VMEM((HEADS, 3 * HD, LEN), BF),
            pltpu.VMEM((SEQ, 3 * HD, LEN), BF),
            pltpu.VMEM((CHUNKS, CHUNK, HD), BF),
            pltpu.VMEM((CHUNKS, CHUNK, HD), BF),
            pltpu.VMEM((CHUNKS, HD, CHUNK), BF),
            pltpu.VMEM((CHUNKS, HD, CHUNK), BF),
            pltpu.VMEM((CHUNKS, HD, LEN), F32),
            pltpu.VMEM((HEADS, HD, LEN), F32),
            pltpu.VMEM((LEN, WIDTH), F32),
            pltpu.VMEM((HEADS, HD, LEN), BF),
            pltpu.VMEM((CHUNKS, HD, LEN), BF),
            pltpu.VMEM((CHUNKS, CHUNK, 2 * HD), F32),
            pltpu.VMEM((CHUNKS, LEN, 2 * HD), F32),
            pltpu.VMEM((CHUNKS, LEN, 2 * HD), BF),
            pltpu.VMEM((HEADS, LEN, 2 * HD), BF),
            pltpu.VMEM((CHUNKS, HD, LEN), BF),
            pltpu.VMEM((HEADS, HD, LEN), BF),
            pltpu.VMEM((2 * LEN, 2 * HD), BF),
            pltpu.SemaphoreType.DMA((4,)),
            pltpu.SemaphoreType.DMA((18,)),
            pltpu.SemaphoreType.DMA((CHUNKS,)),
            pltpu.SemaphoreType.DMA((CHUNKS,)),
            pltpu.SemaphoreType.DMA((CHUNKS,)),
            pltpu.SemaphoreType.DMA((CHUNKS,)),
        ],
        compiler_params=pltpu.CompilerParams(
            collective_id=0, has_side_effects=True, vmem_limit_bytes=VMEM_LIMIT
        ),
        name="layer",
    )(stored[None, :], stored[:, None], length, item_table, input_proj, output_proj, cot)


def sum_kernel(block, want_ref, packed_ref, out_ref, spread_buf, rows_buf):
    j = pl.program_id(0)

    @pl.when(j == 0)
    def _():
        unpack_rows(packed_ref, spread_buf, rows_buf)

    rows = iota((block, OWNERS), 0) + j * block
    pick = jnp.concatenate(
        [(want_ref[r : r + 1, :] == rows).astype(F32).astype(BF) for r in range(CAP)], axis=1
    )
    out_ref[...] = nn(pick, rows_buf[...]).astype(BF)


def sum_rows(wanted, arrived, rows_dev):
    block = 512
    return pl.pallas_call(
        functools.partial(sum_kernel, block),
        out_shape=jax.ShapeDtypeStruct((rows_dev, WIDTH), BF),
        grid=(rows_dev // block,),
        in_specs=[
            pl.BlockSpec((8, OWNERS), lambda j: (0, 0)),
            pl.BlockSpec((OWNERS, PIECES, 128), lambda j: (0, 0, 0)),
        ],
        out_specs=pl.BlockSpec((block, WIDTH), lambda j: (j, 0)),
        scratch_shapes=[
            pltpu.VMEM((OWNERS * PIECES, 128), F32),
            pltpu.VMEM((CAP * OWNERS, WIDTH), BF),
        ],
        compiler_params=pltpu.CompilerParams(vmem_limit_bytes=VMEM_LIMIT),
        name="sums",
    )(wanted, arrived)


def local(item_ids, history_len, row_place, item_table, input_proj, output_proj, out_cotangent):
    stored = row_place[item_ids[0]]
    layer_out, arrived, wanted = layer(
        stored, history_len, item_table, input_proj, output_proj, out_cotangent[0]
    )
    table_grad = sum_rows(wanted, arrived, item_table.shape[0])
    return layer_out[None], table_grad


def solution(mesh):
    placed = (
        P("table", "seq"),
        P("table"),
        P(),
        P(("table", "seq"), None),
        P(),
        P(),
        P("table", "seq", None),
    )
    return jax.shard_map(
        local,
        mesh=mesh,
        in_specs=placed,
        out_specs=(P("table", "seq", None), P(("table", "seq"), None)),
        check_vma=False,
    )
```

time: 152 us -> 128 us (0.84)
  Pallas kernels: 147 us -> 122 us
    pallas_call x2 -> x0, Pallas kernels: 61.8 us -> none  [the longest x1 41.4 us: fetch_rows(): pl.pallas_call(rows_kernel, out_shape=(jax.ShapeDtypeStruct((OWNERS, PIEC...]
    pallas_call x1, Pallas kernels: 77.1 us -> 115 us  [layer(): pl.pallas_call(layer_kernel, out_shape=(jax.ShapeDtypeStruct((LEN, WIDTH)...]
where the time goes in v2:
time: 128 us
  Pallas kernels  122 us (95%)
  local copies, waits for them, and re-layouts  3.35 us (3%)
  between operations  1.47 us (1%)
    pallas_call x1, Pallas kernels, layer(): pl.pallas_call(layer_kernel, out_shape=(jax.ShapeDtypeStruct((LEN, WIDTH)...  115 us
    pallas_call x1, Pallas kernels, sum_rows(): pl.pallas_call(functools.partial(sum_kernel, block), out_shape=jax.ShapeD...  7.66 us

profile of v2, /device:TPU:1, one launch (start us, length us, event | category | flops | bytes accessed | tf_op | source)
XLA Modules:
  0.0 127.9 jit_solution(9749843116154501918)
XLA Ops:
  0.6 0.0 copy-start
  1.4 0.7 compare_select_fusion
  2.1 0.1 copy-done
  2.2 1.7 %gather_fusion = s32[256]{0:T(256)S(1)} fusion(s32[524288]{0:T(1024)S(1)} %copy-done, s32[1024]{0:T(1024)S(1)} %pad_clamp_fusion), kind=kCustom, calls=%fused_computation | custom fusion | bytes 3072 | tf_op jit(solution)/shard_map/gather | solution.py:574
  4.0 0.0 copy-start.2
  4.0 0.8 copy.9.stored_ref
  4.8 0.0 copy-done.2
  4.8 114.7 %layer.1 = (bf16[256,512]{1,0:T(8,128)(2,1)}, bf16[128,24,128]{2,1,0:T(8,128)(2,1)}, s32[8,128]{1,0:T(8,128)}) custom-call(s32[1,256]{1,0:T(1,128)} %bitcast.10, s32[256,1]{1,0:T(8,128)} %copy.9.stored_ref, s32[1]{0:T(128)S(6)} %copy.11.len_ref, bf16[4096,512]{1,0:T(8,128)(2,1)} %table_hbm.1, bf16[512,2048]{1,0:T(8,128)(2,1)} %win_hbm.1, ...), custom_call_target="tpu_custom_call" | custom-call | tf_op jit(solution)/shard_map/layer/pallas_call | solution.py:480
  119.5 0.0 copy-start.1
  119.5 7.7 %sums.1 = bf16[4096,512]{1,0:T(8,128)(2,1)} custom-call(s32[8,128]{1,0:T(8,128)} %get-tuple-element.6.want_ref, bf16[128,24,128]{2,1,0:T(8,128)(2,1)} %get-tuple-element.7.packed_ref), custom_call_target="tpu_custom_call" | custom-call | tf_op jit(solution)/shard_map/sums/pallas_call | solution.py:555
  127.2 0.0 copy-done.1
  127.2 0.7 copy.12
  (1 shorter events, 0.0 us)
Async XLA Ops:
  0.6 1.6 %copy-start = (s32[524288]{0:T(1024)S(1)}, s32[524288]{0:T(1024)}, u32[]{:S(2)}) copy-start(s32[524288]{0:T(1024)} %param.9) | copy-start | bytes 6291460
  4.0 0.8 copy-start.2
  119.5 7.7 %copy-start.1 = (bf16[256,512]{1,0:T(8,128)(2,1)S(1)}, bf16[256,512]{1,0:T(8,128)(2,1)}, u32[]{:S(2)}) copy-start(bf16[256,512]{1,0:T(8,128)(2,1)} %get-tuple-element.5) | copy-start | bytes 786436

commit v3 on v2

--- a/solution.py
+++ b/solution.py
@@ -23,6 +23,7 @@
 PIECES = CAP * WIDTH // 128
 CHUNK = 2 * LEN
 CHUNKS = SEQ // 2
+AHEAD = 3
 VMEM_LIMIT = 56 * 2**20
 
 
@@ -49,18 +50,20 @@
     return (0.5 + 0.5 * th) * (1.0 + u * (1.0 - th))
 
 
-def mean_last(x):
-    return jnp.mean(x, axis=-1, keepdims=True)
-
-
-def normalize(x):
-    centred = x - mean_last(x)
-    spread = jnp.sqrt(mean_last(centred * centred) + EPS)
+def normalize(x, axis=1):
+    def mean(y):
+        return jnp.mean(y, axis=axis, keepdims=True)
+
+    centred = x - mean(x)
+    spread = jnp.sqrt(mean(centred * centred) + EPS)
     return centred / spread, spread
 
 
-def norm_back(gradient, normed, spread):
-    return (gradient - mean_last(gradient) - normed * mean_last(gradient * normed)) / spread
+def norm_back(gradient, normed, spread, axis=1):
+    def mean(y):
+        return jnp.mean(y, axis=axis, keepdims=True)
+
+    return (gradient - mean(gradient) - normed * mean(gradient * normed)) / spread
 
 
 def places():
@@ -128,13 +131,13 @@
 
 
 def layer_kernel(
-    ids_ref, stored_ref, len_ref, table_hbm, win_hbm, wo_hbm, cot_hbm,
+    ids_ref, len_ref, table_hbm, win_hbm, wo_hbm, cot_hbm,
     out_ref, grads_ref, want_ref,
     table_ref, win_ref, wo_ref, cot_ref, all_ids, ids2d, acc, outbuf, ans_ref,
     spread_buf, rows_buf, emb, norm_exact, in_spread, pre, gate, mixed_grad,
     qkv_send, qkv_all, key_nat, value_nat, key_t, value_t,
     o_send, o_all, attn_norm, d_send, d_all,
-    dkv_acc, dkv_peer, dkv_send, dkv_all, dq_send, dq_all, qd_pad,
+    dkv_acc, dkv_peer, dkv_send, dkv_all, dq_send, dq_all, qd_pad, p_ahead, c_ahead,
     load_sem, sem, qkv_sem, relay_sem, d_sem, peer_sem,
 ):
     t, s = places()
@@ -192,7 +195,10 @@
 
     lax.fori_loop(1, TABLE, to_column, 0)
 
-    stored = stored_ref[...]
+    diagonal = iota((LEN, LEN), 0) == iota((LEN, LEN), 1)
+    stored = jnp.sum(
+        jnp.where(diagonal, ids_ref[...].astype(F32), 0.0), axis=1, keepdims=True
+    ).astype(jnp.int32)
     owner = stored // rows_dev
     owned = (iota((LEN, OWNERS), 1) == owner).astype(F32)
     earlier = (iota((LEN, LEN), 1) < iota((LEN, LEN), 0)).astype(BF)
@@ -228,58 +234,52 @@
     half_count = OWNERS // 2
     loads[0].wait()
 
-    def send_group(src_ref, dst_ref, dst_at, send_sem, recv_sem, g):
-        tt = lax.rem(t + g, TABLE)
-
-        def one(i, carry):
-            ss = lax.rem(s + i, SEQ)
-
-            @pl.when((g > 0) | (i > 0))
-            def _():
-                remote(
-                    src_ref.at[g * SEQ + ss], dst_ref.at[dst_at(tt)], send_sem, recv_sem, tt, ss
-                ).start()
-
-            return carry
-
-        lax.fori_loop(0, SEQ, one, 0)
-
+    def send_one(src_ref, dst_ref, dst_at, send_sem, recv_sem, n):
+        tt = lax.rem(t + n // SEQ, TABLE)
+        ss = lax.rem(s + n, SEQ)
+        remote(
+            src_ref.at[n // SEQ * SEQ + ss], dst_ref.at[dst_at(tt)], send_sem, recv_sem, tt, ss
+        ).start()
+
+    def send_row(n):
+        send_one(outbuf, ans_ref, lambda tt: me, sem.at[14], sem.at[15], n)
+
+    steps = rows_dev // block
+    each = half_count // steps
     for half in range(2):
         low = half * half_count
 
-        def gather(j, carry, low=low):
+        def gather(j, carry, half=half, low=low):
             base = j * block
             table_blk = table_ref[pl.ds(pl.multiple_of(base, block), block), :]
             cols = iota((half_count, block), 1) + base
             pick_rows = jnp.concatenate(
                 [(w[low : low + half_count] == cols).astype(F32).astype(BF) for w in wanted], axis=0
             )
+            if half:
+                for n in range(1, each):
+                    send_row(j * each + n)
             part = nn(pick_rows, table_blk)
-
-            @pl.when(j == 0)
-            def _():
-                acc[...] = part
-
-            @pl.when(j > 0)
-            def _():
-                acc[...] += part
-
+            acc[...] += part
             return carry
 
-        lax.fori_loop(0, rows_dev // block, gather, 0)
+        acc[...] = jnp.zeros_like(acc)
+        lax.fori_loop(0, steps, gather, 0)
         pack_rows(acc, half_count, spread_buf, outbuf, low)
 
-        def send_rows(g, carry):
-            send_group(outbuf, ans_ref, lambda tt: me, sem.at[14], sem.at[15], g)
-            return carry
-
-        lax.fori_loop(half * TABLE // 2, (half + 1) * TABLE // 2, send_rows, 0)
+    def send_rest(n, carry):
+        send_row(half_count + n)
+        return carry
+
+    lax.fori_loop(0, half_count, send_rest, 0)
+    for n in range(1, steps):
+        send_row(n * each)
     ans_ref[me] = outbuf[s]
     pick = (iota((LEN, CAP * OWNERS), 1) == slot).astype(F32).astype(BF)
     for load in loads[1:]:
         load.wait()
     cot = jnp.where(live, cot_ref[...].astype(F32), 0.0)
-    mixed_grad[...] = nt(cot.astype(BF), wo_ref[...])
+    mixed_grad[...] = nt(wo_ref[...], cot.astype(BF))
     dkv_acc[...] = jnp.zeros_like(dkv_acc)
     qd_pad[...] = jnp.zeros_like(qd_pad)
     wait_bytes(ans_ref.at[pl.ds(0, OWNERS - 1)], sem.at[15])
@@ -309,7 +309,7 @@
 
     lax.fori_loop(0, HEADS, send_qkv, 0)
 
-    gate[...] = silu(pre[:, :WIDTH])
+    gate[...] = silu(pre[:, :WIDTH]).T
     pre[...] = dsilu(pre[...])
 
     peer = plane + 1 - core
@@ -320,15 +320,16 @@
         ref = qkv_all.at[i, pl.ds(HD, 2 * HD)]
         remote(ref, ref, sem.at[1], relay_sem.at[k], peer, s).start()
 
-    relay(0)
+    for k in range(AHEAD):
+        relay(k)
 
     def may_see(k):
         offset = lax.rem(k + core, 2) * LEN
         return iota((CHUNK, LEN), 0) <= iota((CHUNK, LEN), 1) + offset
 
     for k in range(CHUNKS):
-        if k < CHUNKS - 1:
-            relay(k + 1)
+        if k + AHEAD < CHUNKS:
+            relay(k + AHEAD)
         wait_bytes(qkv_all.at[0, pl.ds(HD, 2 * HD)], relay_sem.at[k])
         for half in range(2):
             both = qkv_all[2 * k + half]
@@ -351,14 +352,34 @@
             owner_t, query_block(core, k),
         )
 
+    def score_terms(k, j):
+        u = nn(key_nat[j], qkv_all[query_block(core, k), :HD])
+        th = jnp.tanh(u)
+        a = 1.0 + th
+        p = u * a
+        c = a * (1.0 + u * (1.0 - th))
+        if j == k:
+            p = jnp.where(may_see(k), p, 0.0)
+            c = jnp.where(may_see(k), c, 0.0)
+        return p.astype(BF), c
+
+    def score_ahead(k):
+        for j in range(k + 1):
+            p, c = score_terms(k, j)
+            p_ahead[CHUNKS - 1 - k, j] = p
+            c_ahead[CHUNKS - 1 - k, j] = c
+
+    score_ahead(CHUNKS - 1)
+
     wait_bytes(o_all, sem.at[3])
-    attention = o_all[...].reshape(WIDTH, LEN).T
-    attention = jnp.where(live, attention, 0.0)
-    attn, attn_spread = normalize(attention)
+    attention = o_all[...].reshape(WIDTH, LEN)
+    live_lanes = s * LEN + iota((1, LEN), 1) < len_ref[0]
+    attention = jnp.where(live_lanes, attention, 0.0)
+    attn, attn_spread = normalize(attention, 0)
     attn_norm[...] = attn
     dz = mixed_grad[...] * gate[...]
-    attention_grad = norm_back(dz, attn, attn_spread).astype(BF).astype(F32)
-    d_send[...] = (0.5 * attention_grad).T.astype(BF).reshape(HEADS, HD, LEN)
+    attention_grad = norm_back(dz, attn, attn_spread, 0).astype(BF).astype(F32)
+    d_send[...] = (0.5 * attention_grad).astype(BF).reshape(HEADS, HD, LEN)
 
     def send_d(i, carry):
         h = lax.rem(i + s, HEADS)
@@ -369,9 +390,11 @@
         return carry
 
     lax.fori_loop(0, HEADS, send_d, 0)
-    mixed = (attn * gate[...]).astype(BF)
+    mixed = (attn_norm[...] * gate[...]).T.astype(BF)
     branch = nn(mixed, wo_ref[...])
     out_ref[...] = jnp.where(live, emb[...] + branch, 0.0).astype(BF)
+
+    score_ahead(CHUNKS - 2)
 
     def reduce_keys(k):
         wait_bytes(dkv_peer.at[k], peer_sem.at[k])
@@ -396,17 +419,11 @@
         pair = qd_pad[...]
         total = None
         for j in range(k + 1):
-            u = nn(key_nat[j], query)
-            dp = nn(value_nat[j], grad)
-            th = jnp.tanh(u)
-            a = 1.0 + th
-            p = u * a
-            ds = dp * (a * (1.0 + u * (1.0 - th)))
-            if j == k:
-                p = jnp.where(may_see(k), p, 0.0)
-                ds = jnp.where(may_see(k), ds, 0.0)
-            p = p.astype(BF)
-            ds = ds.astype(BF)
+            if k >= CHUNKS - 2:
+                p, c = p_ahead[CHUNKS - 1 - k, j], c_ahead[CHUNKS - 1 - k, j]
+            else:
+                p, c = score_terms(k, j)
+            ds = (nn(value_nat[j], grad) * c).astype(BF)
             dkv_acc[j] += nn(ds, pair[:LEN]) + nn(p, pair[LEN:])
             part = nn(key_t[j], ds)
             total = part if total is None else total + part
@@ -429,7 +446,7 @@
             [dkv_all[h][:, low : low + HD].astype(F32) for h in range(HEADS)], axis=1
         )
 
-    norm_grad = back(0, mixed_grad[...] * attn_norm[...])
+    norm_grad = back(0, (mixed_grad[...] * attn_norm[...]).T)
     wait_bytes(dq_all, sem.at[8])
     norm_grad += back(2, dq_all[...].reshape(WIDTH, LEN).astype(F32).T)
     wait_bytes(dkv_all, sem.at[6])
@@ -446,14 +463,14 @@
     )
     pack_rows(acc_put, OWNERS, spread_buf, outbuf, 0)
 
-    def send_grads(g, carry):
-        send_group(
+    def send_grads(n, carry):
+        send_one(
             outbuf, grads_ref, lambda tt: lax.rem(t - tt + TABLE, TABLE) * SEQ + s,
-            sem.at[16], sem.at[17], g,
-        )
-        return carry
-
-    lax.fori_loop(0, TABLE, send_grads, 0)
+            sem.at[16], sem.at[17], n,
+        )
+        return carry
+
+    lax.fori_loop(1, OWNERS, send_grads, 0)
     grads_ref[s] = outbuf[s]
 
     wait_bytes(all_ids.at[pl.ds(0, SEQ - 1)], sem.at[10])
@@ -484,7 +501,7 @@
             jax.ShapeDtypeStruct((OWNERS, PIECES, 128), BF),
             jax.ShapeDtypeStruct((8, OWNERS), jnp.int32),
         ),
-        in_specs=[VM, VM, SM, anywhere, anywhere, anywhere, anywhere],
+        in_specs=[VM, SM, anywhere, anywhere, anywhere, anywhere],
         out_specs=(VM, VM, VM),
         scratch_shapes=[
             pltpu.VMEM(item_table.shape, BF),
@@ -502,8 +519,8 @@
             pltpu.VMEM((LEN, WIDTH), F32),
             pltpu.VMEM((LEN, 128), F32),
             pltpu.VMEM((LEN, 4 * WIDTH), F32),
-            pltpu.VMEM((LEN, WIDTH), F32),
-            pltpu.VMEM((LEN, WIDTH), F32),
+            pltpu.VMEM((WIDTH, LEN), F32),
+            pltpu.VMEM((WIDTH, LEN), F32),
             pltpu.VMEM((HEADS, 3 * HD, LEN), BF),
             pltpu.VMEM((SEQ, 3 * HD, LEN), BF),
             pltpu.VMEM((CHUNKS, CHUNK, HD), BF),
@@ -512,7 +529,7 @@
             pltpu.VMEM((CHUNKS, HD, CHUNK), BF),
             pltpu.VMEM((CHUNKS, HD, LEN), F32),
             pltpu.VMEM((HEADS, HD, LEN), F32),
-            pltpu.VMEM((LEN, WIDTH), F32),
+            pltpu.VMEM((WIDTH, LEN), F32),
             pltpu.VMEM((HEADS, HD, LEN), BF),
             pltpu.VMEM((CHUNKS, HD, LEN), BF),
             pltpu.VMEM((CHUNKS, CHUNK, 2 * HD), F32),
@@ -522,6 +539,8 @@
             pltpu.VMEM((CHUNKS, HD, LEN), BF),
             pltpu.VMEM((HEADS, HD, LEN), BF),
             pltpu.VMEM((2 * LEN, 2 * HD), BF),
+            pltpu.VMEM((2, CHUNKS, CHUNK, LEN), BF),
+            pltpu.VMEM((2, CHUNKS, CHUNK, LEN), F32),
             pltpu.SemaphoreType.DMA((4,)),
             pltpu.SemaphoreType.DMA((18,)),
             pltpu.SemaphoreType.DMA((CHUNKS,)),
@@ -533,16 +552,17 @@
             collective_id=0, has_side_effects=True, vmem_limit_bytes=VMEM_LIMIT
         ),
         name="layer",
-    )(stored[None, :], stored[:, None], length, item_table, input_proj, output_proj, cot)
-
-
-def sum_kernel(block, want_ref, packed_ref, out_ref, spread_buf, rows_buf):
+    )(stored[None, :], length, item_table, input_proj, output_proj, cot)
+
+
+def sum_kernel(block, want_ref, packed_ref, layer_ref, out_ref, same_ref, spread_buf, rows_buf):
     j = pl.program_id(0)
 
     @pl.when(j == 0)
     def _():
         unpack_rows(packed_ref, spread_buf, rows_buf)
 
+    same_ref[...] = layer_ref[...]
     rows = iota((block, OWNERS), 0) + j * block
     pick = jnp.concatenate(
         [(want_ref[r : r + 1, :] == rows).astype(F32).astype(BF) for r in range(CAP)], axis=1
@@ -550,32 +570,40 @@
     out_ref[...] = nn(pick, rows_buf[...]).astype(BF)
 
 
-def sum_rows(wanted, arrived, rows_dev):
+def sum_rows(wanted, arrived, layer_out, rows_dev):
     block = 512
+    part = LEN * block // rows_dev
     return pl.pallas_call(
         functools.partial(sum_kernel, block),
-        out_shape=jax.ShapeDtypeStruct((rows_dev, WIDTH), BF),
+        out_shape=(
+            jax.ShapeDtypeStruct((rows_dev, WIDTH), BF),
+            jax.ShapeDtypeStruct((LEN, WIDTH), BF),
+        ),
         grid=(rows_dev // block,),
         in_specs=[
             pl.BlockSpec((8, OWNERS), lambda j: (0, 0)),
             pl.BlockSpec((OWNERS, PIECES, 128), lambda j: (0, 0, 0)),
+            pl.BlockSpec((part, WIDTH), lambda j: (j, 0)),
         ],
-        out_specs=pl.BlockSpec((block, WIDTH), lambda j: (j, 0)),
+        out_specs=(
+            pl.BlockSpec((block, WIDTH), lambda j: (j, 0)),
+            pl.BlockSpec((part, WIDTH), lambda j: (j, 0)),
+        ),
         scratch_shapes=[
             pltpu.VMEM((OWNERS * PIECES, 128), F32),
             pltpu.VMEM((CAP * OWNERS, WIDTH), BF),
         ],
         compiler_params=pltpu.CompilerParams(vmem_limit_bytes=VMEM_LIMIT),
         name="sums",
-    )(wanted, arrived)
+    )(wanted, arrived, layer_out)
 
 
 def local(item_ids, history_len, row_place, item_table, input_proj, output_proj, out_cotangent):
-    stored = row_place[item_ids[0]]
+    stored = row_place.at[item_ids[0]].get(mode="promise_in_bounds")
     layer_out, arrived, wanted = layer(
         stored, history_len, item_table, input_proj, output_proj, out_cotangent[0]
     )
-    table_grad = sum_rows(wanted, arrived, item_table.shape[0])
+    table_grad, layer_out = sum_rows(wanted, arrived, layer_out, item_table.shape[0])
     return layer_out[None], table_grad
 
 

time: 128 us -> 125 us (0.977)
  Pallas kernels: 122 us -> 120 us
    pallas_call x1, Pallas kernels: 115 us -> 112 us  [layer(): pl.pallas_call(layer_kernel, out_shape=(jax.ShapeDtypeStruct((LEN, WIDTH)...]
where the time goes in v3:
time: 125 us; the launch traced here: 124 us
  Pallas kernels  120 us (96%)
  local copies, waits for them, and re-layouts  2.43 us (2%)
  between operations  1.44 us (1%)
    pallas_call x1, Pallas kernels, layer(): pl.pallas_call(layer_kernel, out_shape=(jax.ShapeDtypeStruct((LEN, WIDTH)...  112 us
    pallas_call x1, Pallas kernels, sum_rows(): pl.pallas_call(functools.partial(sum_kernel, block), out_shape=(jax.Shape...  7.92 us

profile of v3, /device:TPU:1, one launch (start us, length us, event | category | flops | bytes accessed | tf_op | source)
XLA Modules:
  0.0 124.4 jit_solution(9552274415642063957)
XLA Ops:
  0.6 0.0 copy-start
  1.4 0.7 compare_select_fusion
  2.1 0.1 copy-done
  2.2 2.3 %gather_fusion = s32[256]{0:T(256)} fusion(s32[524288]{0:T(1024)S(1)} %copy-done, s32[1024]{0:T(1024)S(1)} %pad_clamp_fusion), kind=kCustom, calls=%fused_computation | custom fusion | bytes 3072 | tf_op jit(solution)/shard_map/gather | solution.py:602
  4.6 111.9 %layer.1 = (bf16[256,512]{1,0:T(8,128)(2,1)}, bf16[128,24,128]{2,1,0:T(8,128)(2,1)}, s32[8,128]{1,0:T(8,128)}) custom-call(s32[1,256]{1,0:T(1,128)} %bitcast.8, s32[1]{0:T(128)S(6)} %copy.9.len_ref, bf16[4096,512]{1,0:T(8,128)(2,1)} %table_hbm.1, bf16[512,2048]{1,0:T(8,128)(2,1)} %win_hbm.1, bf16[512,512]{1,0:T(8,128)(2,1)} %wo_hbm.1, bf16[256,512]{1,0:T(8,128)(2,1)} %bitcast.6), custom_call_target="tpu_custom_call" | custom-call | tf_op jit(solution)/shard_map/layer/pallas_call | solution.py:497
  116.5 7.9 %sums.1 = (bf16[4096,512]{1,0:T(8,128)(2,1)}, bf16[256,512]{1,0:T(8,128)(2,1)}) custom-call(s32[8,128]{1,0:T(8,128)} %get-tuple-element.7.want_ref, bf16[128,24,128]{2,1,0:T(8,128)(2,1)} %get-tuple-element.8.packed_ref, bf16[256,512]{1,0:T(8,128)(2,1)} %get-tuple-element.9.layer_ref), custom_call_target="tpu_custom_call" | custom-call | tf_op jit(solution)/shard_map/sums/pallas_call | solution.py:576
  (1 shorter events, 0.0 us)
Async XLA Ops:
  0.6 1.6 %copy-start = (s32[524288]{0:T(1024)S(1)}, s32[524288]{0:T(1024)}, u32[]{:S(2)}) copy-start(s32[524288]{0:T(1024)} %param.9) | copy-start | bytes 6291460

commit v4 on v3

--- a/solution.py
+++ b/solution.py
@@ -72,7 +72,7 @@
     return t, s
 
 
-def barrier_all():
+def greet_all():
     t, s = places()
     me = t * SEQ + s
     sem = pltpu.get_barrier_semaphore()
@@ -85,7 +85,10 @@
         return carry
 
     lax.fori_loop(1, OWNERS, body, 0)
-    pl.semaphore_wait(sem, OWNERS - 1)
+
+
+def wait_all():
+    pl.semaphore_wait(pltpu.get_barrier_semaphore(), OWNERS - 1)
 
 
 def remote(src, dst, send_sem, recv_sem, t, s):
@@ -131,9 +134,9 @@
 
 
 def layer_kernel(
-    ids_ref, len_ref, table_hbm, win_hbm, wo_hbm, cot_hbm,
+    ids_ref, len_ref, place_hbm, table_hbm, win_hbm, wo_hbm, cot_hbm,
     out_ref, grads_ref, want_ref,
-    table_ref, win_ref, wo_ref, cot_ref, all_ids, ids2d, acc, outbuf, ans_ref,
+    place_ref, look, table_ref, win_ref, wo_ref, cot_ref, all_ids, ids2d, acc, outbuf, ans_ref,
     spread_buf, rows_buf, emb, norm_exact, in_spread, pre, gate, mixed_grad,
     qkv_send, qkv_all, key_nat, value_nat, key_t, value_t,
     o_send, o_all, attn_norm, d_send, d_all,
@@ -155,13 +158,41 @@
     loads = [
         pltpu.make_async_copy(src, dst, load_sem.at[n])
         for n, (src, dst) in enumerate(
-            ((table_hbm, table_ref), (win_hbm, win_ref), (wo_hbm, wo_ref), (cot_hbm, cot_ref))
+            ((place_hbm, place_ref), (table_hbm, table_ref), (win_hbm, win_ref), (wo_hbm, wo_ref), (cot_hbm, cot_ref))
         )
     ]
     for load in loads:
         load.start()
-    all_ids[me] = ids_ref[...]
-    barrier_all()
+    greet_all()
+
+    diagonal = iota((LEN, LEN), 0) == iota((LEN, LEN), 1)
+    items = jnp.sum(
+        jnp.where(diagonal, ids_ref[...].astype(F32), 0.0), axis=1, keepdims=True
+    ).astype(jnp.int32)
+    line = items // 128
+    look[...] = jnp.zeros_like(look)
+    loads[0].wait()
+    lines = 512
+
+    def look_up(j, carry):
+        base = j * lines
+        places_blk = place_ref[pl.ds(pl.multiple_of(base, lines), lines), :]
+        digits = jnp.concatenate(
+            [((places_blk >> (7 * n)) & 127).astype(F32).astype(BF) for n in range(3)], axis=1
+        )
+        chosen = (line == iota((LEN, lines), 1) + base).astype(F32).astype(BF)
+        look[...] += nn(chosen, digits)
+        return carry
+
+    lax.fori_loop(0, place_ref.shape[0] // lines, look_up, 0)
+    found = look[:, :128] + 128.0 * look[:, 128:256] + 16384.0 * look[:, 256:]
+    mine_at = iota((LEN, 128), 1) == lax.rem(items, 128)
+    stored_f = jnp.sum(jnp.where(mine_at, found, 0.0), axis=1, keepdims=True)
+    stored = stored_f.astype(jnp.int32)
+    all_ids[me] = jnp.sum(
+        jnp.where(diagonal, stored_f, 0.0), axis=0, keepdims=True
+    ).astype(jnp.int32)
+    wait_all()
 
     def send(src, dst, send_sem, recv_sem, tt, ss):
         local = (tt == t) & (ss == s)
@@ -195,10 +226,6 @@
 
     lax.fori_loop(1, TABLE, to_column, 0)
 
-    diagonal = iota((LEN, LEN), 0) == iota((LEN, LEN), 1)
-    stored = jnp.sum(
-        jnp.where(diagonal, ids_ref[...].astype(F32), 0.0), axis=1, keepdims=True
-    ).astype(jnp.int32)
     owner = stored // rows_dev
     owned = (iota((LEN, OWNERS), 1) == owner).astype(F32)
     earlier = (iota((LEN, LEN), 1) < iota((LEN, LEN), 0)).astype(BF)
@@ -231,8 +258,9 @@
     want_ref[...] = square.T[:8].astype(jnp.int32)
 
     block = 512
-    half_count = OWNERS // 2
-    loads[0].wait()
+    parts = 2
+    count = OWNERS // parts
+    loads[1].wait()
 
     def send_one(src_ref, dst_ref, dst_at, send_sem, recv_sem, n):
         tt = lax.rem(t + n // SEQ, TABLE)
@@ -245,38 +273,37 @@
         send_one(outbuf, ans_ref, lambda tt: me, sem.at[14], sem.at[15], n)
 
     steps = rows_dev // block
-    each = half_count // steps
-    for half in range(2):
-        low = half * half_count
-
-        def gather(j, carry, half=half, low=low):
+    each = count // steps
+    for part in range(parts):
+        low = part * count
+
+        def gather(j, carry, part=part, low=low):
             base = j * block
             table_blk = table_ref[pl.ds(pl.multiple_of(base, block), block), :]
-            cols = iota((half_count, block), 1) + base
+            cols = iota((count, block), 1) + base
             pick_rows = jnp.concatenate(
-                [(w[low : low + half_count] == cols).astype(F32).astype(BF) for w in wanted], axis=0
+                [(w[low : low + count] == cols).astype(F32).astype(BF) for w in wanted], axis=0
             )
-            if half:
-                for n in range(1, each):
-                    send_row(j * each + n)
-            part = nn(pick_rows, table_blk)
-            acc[...] += part
+            if part:
+                for n in range(1 if part == 1 else 0, each):
+                    send_row(low - count + j * each + n)
+            acc[...] += nn(pick_rows, table_blk)
             return carry
 
         acc[...] = jnp.zeros_like(acc)
         lax.fori_loop(0, steps, gather, 0)
-        pack_rows(acc, half_count, spread_buf, outbuf, low)
+        pack_rows(acc, count, spread_buf, outbuf, low)
 
     def send_rest(n, carry):
-        send_row(half_count + n)
-        return carry
-
-    lax.fori_loop(0, half_count, send_rest, 0)
+        send_row(OWNERS - count + n)
+        return carry
+
+    lax.fori_loop(0, count, send_rest, 0)
     for n in range(1, steps):
         send_row(n * each)
     ans_ref[me] = outbuf[s]
     pick = (iota((LEN, CAP * OWNERS), 1) == slot).astype(F32).astype(BF)
-    for load in loads[1:]:
+    for load in loads[2:]:
         load.wait()
     cot = jnp.where(live, cot_ref[...].astype(F32), 0.0)
     mixed_grad[...] = nt(wo_ref[...], cot.astype(BF))
@@ -456,21 +483,37 @@
     embed_grad = cot + norm_back(norm_grad, norm_exact[...], in_spread[:, :1])
     wait_bytes(outbuf.at[pl.ds(0, OWNERS - 1)], sem.at[14])
     turned_owner = lax.rem(owner + (OWNERS - t * SEQ), OWNERS)
-    turned_slot = rank.astype(jnp.int32) * OWNERS + turned_owner
-    put_pick = (iota((LEN, CAP * OWNERS), 1) == turned_slot).astype(F32).astype(BF)
-    acc_put = lax.dot_general(
-        put_pick, embed_grad.astype(BF), (((0,), (0,)), ((), ())), preferred_element_type=F32
+    some = CAP * count
+    turned_slot = (
+        turned_owner // count * some
+        + rank.astype(jnp.int32) * count
+        + lax.rem(turned_owner, count)
     )
-    pack_rows(acc_put, OWNERS, spread_buf, outbuf, 0)
-
-    def send_grads(n, carry):
+    embed_grad = embed_grad.astype(BF)
+
+    def send_grad(n):
         send_one(
             outbuf, grads_ref, lambda tt: lax.rem(t - tt + TABLE, TABLE) * SEQ + s,
             sem.at[16], sem.at[17], n,
         )
-        return carry
-
-    lax.fori_loop(1, OWNERS, send_grads, 0)
+
+    for part in range(parts):
+        chosen = (iota((LEN, some), 1) + part * some == turned_slot).astype(F32).astype(BF)
+        put = lax.dot_general(
+            chosen, embed_grad, (((0,), (0,)), ((), ())), preferred_element_type=F32
+        )
+        if part:
+            for n in range(1, count):
+                send_grad((part - 1) * count + n)
+        pack_rows(put, count, spread_buf, outbuf, part * count)
+    for part in range(1, parts - 1):
+        send_grad(part * count)
+
+    def send_last(n, carry):
+        send_grad(OWNERS - count + n)
+        return carry
+
+    lax.fori_loop(0, count, send_last, 0)
     grads_ref[s] = outbuf[s]
 
     wait_bytes(all_ids.at[pl.ds(0, SEQ - 1)], sem.at[10])
@@ -492,8 +535,9 @@
     wait_bytes(outbuf.at[pl.ds(0, OWNERS - 1)], sem.at[16])
 
 
-def layer(stored, length, item_table, input_proj, output_proj, cot):
+def layer(item_ids, length, row_place, item_table, input_proj, output_proj, cot):
     anywhere = pl.BlockSpec(memory_space=pl.ANY)
+    lines = row_place.reshape(-1, 128)
     return pl.pallas_call(
         layer_kernel,
         out_shape=(
@@ -501,9 +545,11 @@
             jax.ShapeDtypeStruct((OWNERS, PIECES, 128), BF),
             jax.ShapeDtypeStruct((8, OWNERS), jnp.int32),
         ),
-        in_specs=[VM, SM, anywhere, anywhere, anywhere, anywhere],
+        in_specs=[VM, SM, anywhere, anywhere, anywhere, anywhere, anywhere],
         out_specs=(VM, VM, VM),
         scratch_shapes=[
+            pltpu.VMEM(lines.shape, jnp.int32),
+            pltpu.VMEM((LEN, 3 * 128), F32),
             pltpu.VMEM(item_table.shape, BF),
             pltpu.VMEM((WIDTH, 4 * WIDTH), BF),
             pltpu.VMEM((WIDTH, WIDTH), BF),
@@ -541,7 +587,7 @@
             pltpu.VMEM((2 * LEN, 2 * HD), BF),
             pltpu.VMEM((2, CHUNKS, CHUNK, LEN), BF),
             pltpu.VMEM((2, CHUNKS, CHUNK, LEN), F32),
-            pltpu.SemaphoreType.DMA((4,)),
+            pltpu.SemaphoreType.DMA((5,)),
             pltpu.SemaphoreType.DMA((18,)),
             pltpu.SemaphoreType.DMA((CHUNKS,)),
             pltpu.SemaphoreType.DMA((CHUNKS,)),
@@ -552,7 +598,7 @@
             collective_id=0, has_side_effects=True, vmem_limit_bytes=VMEM_LIMIT
         ),
         name="layer",
-    )(stored[None, :], length, item_table, input_proj, output_proj, cot)
+    )(item_ids, length, lines, item_table, input_proj, output_proj, cot)
 
 
 def sum_kernel(block, want_ref, packed_ref, layer_ref, out_ref, same_ref, spread_buf, rows_buf):
@@ -599,9 +645,8 @@
 
 
 def local(item_ids, history_len, row_place, item_table, input_proj, output_proj, out_cotangent):
-    stored = row_place.at[item_ids[0]].get(mode="promise_in_bounds")
     layer_out, arrived, wanted = layer(
-        stored, history_len, item_table, input_proj, output_proj, out_cotangent[0]
+        item_ids, history_len, row_place, item_table, input_proj, output_proj, out_cotangent[0]
     )
     table_grad, layer_out = sum_rows(wanted, arrived, layer_out, item_table.shape[0])
     return layer_out[None], table_grad

time: 125 us -> 122 us (0.976)
  local copies, waits for them, and re-layouts: 2.43 us -> 0 us
    gather x1 -> x0, local copies, waits for them, and re-layouts: 2.31 us -> none  [local(): stored = row_place.at[item_ids[0]].get(mode='promise_in_bounds')]
where the time goes in v4:
time: 122 us; the launch traced here: 121 us
  Pallas kernels  120 us (98%)
  between operations  1.29 us (1%)
    pallas_call x1, Pallas kernels, layer(): pl.pallas_call(layer_kernel, out_shape=(jax.ShapeDtypeStruct((LEN, WIDTH)...  112 us
    pallas_call x1, Pallas kernels, sum_rows(): pl.pallas_call(functools.partial(sum_kernel, block), out_shape=(jax.Shape...  7.92 us

profile of v4, /device:TPU:1, one launch (start us, length us, event | category | flops | bytes accessed | tf_op | source)
XLA Modules:
  0.0 121.3 jit_solution(13590637196487449469)
XLA Ops:
  1.3 112.1 %layer.1 = (bf16[256,512]{1,0:T(8,128)(2,1)}, bf16[128,24,128]{2,1,0:T(8,128)(2,1)}, s32[8,128]{1,0:T(8,128)}) custom-call(s32[1,256]{1,0:T(1,128)} %ids_ref.1, s32[1]{0:T(128)S(6)} %copy.9.len_ref, s32[4096,128]{1,0:T(8,128)} %bitcast.3, bf16[4096,512]{1,0:T(8,128)(2,1)} %table_hbm.1, bf16[512,2048]{1,0:T(8,128)(2,1)} %win_hbm.1, bf16[512,512]{1,0:T(8,128)(2,1)} %wo_hbm.1, ...), custom_call_target="tpu_custom_call" | custom-call | tf_op jit(solution)/shard_map/layer/pallas_call | solution.py:541
  113.3 7.9 %sums.1 = (bf16[4096,512]{1,0:T(8,128)(2,1)}, bf16[256,512]{1,0:T(8,128)(2,1)}) custom-call(s32[8,128]{1,0:T(8,128)} %get-tuple-element.7.want_ref, bf16[128,24,128]{2,1,0:T(8,128)(2,1)} %get-tuple-element.8.packed_ref, bf16[256,512]{1,0:T(8,128)(2,1)} %get-tuple-element.9.layer_ref), custom_call_target="tpu_custom_call" | custom-call | tf_op jit(solution)/shard_map/sums/pallas_call | solution.py:622

commit v5 on v4

--- a/solution.py
+++ b/solution.py
@@ -373,7 +373,15 @@
                 u = jnp.where(may_see(k), u, 0.0)
             part = nn(value_t[j], (u + u * jnp.tanh(u)).astype(BF))
             total = part if total is None else total + part
-        o_send[k] = total
+        level = jnp.mean(total, axis=0, keepdims=True)
+        o_send[k, :HD, :] = (total - level).astype(BF)
+        row = iota((HD // 4, LEN), 0)
+        terms = jnp.zeros((HD // 4, LEN), F32)
+        for n in range(3):
+            term = level.astype(BF).astype(F32)
+            terms = jnp.where(row == n, term, terms)
+            level = level - term
+        o_send[k, HD:, :] = terms.astype(BF)
         send(
             o_send.at[k], o_all.at[head], sem.at[2], sem.at[3],
             owner_t, query_block(core, k),
@@ -399,7 +407,13 @@
     score_ahead(CHUNKS - 1)
 
     wait_bytes(o_all, sem.at[3])
-    attention = o_all[...].reshape(WIDTH, LEN)
+    attention = jnp.concatenate(
+        [
+            o_all[h, :HD].astype(F32) + jnp.sum(o_all[h, HD:].astype(F32), axis=0, keepdims=True)
+            for h in range(HEADS)
+        ],
+        axis=0,
+    )
     live_lanes = s * LEN + iota((1, LEN), 1) < len_ref[0]
     attention = jnp.where(live_lanes, attention, 0.0)
     attn, attn_spread = normalize(attention, 0)
@@ -573,8 +587,8 @@
             pltpu.VMEM((CHUNKS, CHUNK, HD), BF),
             pltpu.VMEM((CHUNKS, HD, CHUNK), BF),
             pltpu.VMEM((CHUNKS, HD, CHUNK), BF),
-            pltpu.VMEM((CHUNKS, HD, LEN), F32),
-            pltpu.VMEM((HEADS, HD, LEN), F32),
+            pltpu.VMEM((CHUNKS, HD + HD // 4, LEN), BF),
+            pltpu.VMEM((HEADS, HD + HD // 4, LEN), BF),
             pltpu.VMEM((WIDTH, LEN), F32),
             pltpu.VMEM((HEADS, HD, LEN), BF),
             pltpu.VMEM((CHUNKS, HD, LEN), BF),
@@ -617,7 +631,7 @@
 
 
 def sum_rows(wanted, arrived, layer_out, rows_dev):
-    block = 512
+    block = 1024
     part = LEN * block // rows_dev
     return pl.pallas_call(
         functools.partial(sum_kernel, block),

time: 122 us -> 118 us (0.967)
  Pallas kernels: 120 us -> 117 us
    pallas_call x1, Pallas kernels: 112 us -> 110 us  [layer(): pl.pallas_call(layer_kernel, out_shape=(jax.ShapeDtypeStruct((LEN, WIDTH)...]
    pallas_call x1, Pallas kernels: 7.92 us -> 6.55 us  [sum_rows(): pl.pallas_call(functools.partial(sum_kernel, block), out_shape=(jax.Shape...]
where the time goes in v5:
time: 118 us
  Pallas kernels  117 us (99%)
  between operations  1.29 us (1%)
    pallas_call x1, Pallas kernels, layer(): pl.pallas_call(layer_kernel, out_shape=(jax.ShapeDtypeStruct((LEN, WIDTH)...  110 us
    pallas_call x1, Pallas kernels, sum_rows(): pl.pallas_call(functools.partial(sum_kernel, block), out_shape=(jax.Shape...  6.55 us

profile of v5, /device:TPU:1, one launch (start us, length us, event | category | flops | bytes accessed | tf_op | source)
XLA Modules:
  0.0 118.2 jit_solution(7100135007878428619)
XLA Ops:
  1.3 110.4 %layer.1 = (bf16[256,512]{1,0:T(8,128)(2,1)}, bf16[128,24,128]{2,1,0:T(8,128)(2,1)}, s32[8,128]{1,0:T(8,128)}) custom-call(s32[1,256]{1,0:T(1,128)} %ids_ref.1, s32[1]{0:T(128)S(6)} %copy.9.len_ref, s32[4096,128]{1,0:T(8,128)} %bitcast.3, bf16[4096,512]{1,0:T(8,128)(2,1)} %table_hbm.1, bf16[512,2048]{1,0:T(8,128)(2,1)} %win_hbm.1, bf16[512,512]{1,0:T(8,128)(2,1)} %wo_hbm.1, ...), custom_call_target="tpu_custom_call" | custom-call | tf_op jit(solution)/shard_map/layer/pallas_call | solution.py:555
  111.7 6.6 %sums.1 = (bf16[4096,512]{1,0:T(8,128)(2,1)}, bf16[256,512]{1,0:T(8,128)(2,1)}) custom-call(s32[8,128]{1,0:T(8,128)} %get-tuple-element.7.want_ref, bf16[128,24,128]{2,1,0:T(8,128)(2,1)} %get-tuple-element.8.packed_ref, bf16[256,512]{1,0:T(8,128)(2,1)} %get-tuple-element.9.layer_ref), custom_call_target="tpu_custom_call" | custom-call | tf_op jit(solution)/shard_map/sums/pallas_call | solution.py:636
